TPU v7x, 512 devices: a whole 4x4x16 slice. The times are simulated.
512 devices in a mesh: member: 4 (over y), lat: 8 (over x, core), lon: 16 (over z).
Axes of the slice: x: 4, y: 4, z: 16, core: 2. Of those that a mesh axis runs over, the one named last changes fastest.
Arguments:
- ice_flux: float32 [32, 256, 8, 512], P(('member', 'lat'), 'lon'), parts along dimension 0, may hold values from 0.5 to 1.5
- ice_frac: float32 [32, 256, 512], P(('member', 'lat'), 'lon'), parts along dimension 0, may hold values from 0.05 to 1
- ice_mask: int32 [32, 256, 512], P(('member', 'lat'), 'lon'), parts along dimension 0, may hold values 0 or 1
- ice_area: float32 [32, 256, 512], P(('member', 'lat'), 'lon'), parts along dimension 0, may hold values from 0.7 to 44.3
- route: int32 [32, 256], P(('member', 'lat'), 'lon'), parts along dimension 0, may hold values from 0 to 255, as said below
- ocean_area: float32 [2048, 2048], P(('member', 'lat'), 'lon'), parts along dimension 0, may hold values from 0.7 to 44.3
- ocean_wet: int32 [2048, 2048], P(('member', 'lat'), 'lon'), parts along dimension 0, may hold values 0 or 1
- exponent: int32 [8], replicated, may hold values from 0 to 3
Outputs:
- ocean_flux: float32 [8, 2048, 2048], P(None, ('member', 'lat'), 'lon'), parts along dimension 1
- source_total: float32 [32], P('member'), parts along dimension 0
There are 4 independent parts, one for each index of `member`. A program takes and returns all parts, laid end to end along the dimension named above; an argument that names none is the same for every part. Nothing has to cross between parts.
Inputs may be any that keep to these rules, and one draw needn't show every extreme that they name: Within each latitude tile row, route is a permutation of 0 to 255. The 16 entries of one device name, for every longitude tile k that they name (route // 16 == k), exactly 2 blocks of it.
All inputs are finite; a program needn't handle non-finite values. No bound on the sum of `ice_mask` or of `ocean_wet` on one device may be relied on, other than what follows from the above.
Results may differ from a plain program's by a relative error of at most 0.0003.
Values sent between devices are 32-bit elements; how exact they have to be, the bound alone decides.
No kernel may reach another device: no remote copies, remote signals or barrier semaphores. Data moves between devices by JAX's collectives and lax.ppermute only.
A program may use at most 64 MiB of HBM per device.

v0:
```python
import functools

import jax
import jax.numpy as jnp
from jax import lax
from jax.sharding import Mesh
from jax.sharding import PartitionSpec as P

LAT_LON = ("lat_0", "lat_1", "lon")
MEMBER_LAT = ("member", "lat_0", "lat_1")


quantum = 1024.0
limb_base = 65536


def sent_together(arrays, axis, split_dim, concat_dim, along):
    columns = [a.reshape(*a.shape[:along], -1) for a in arrays]
    both = jnp.concatenate(columns, axis=along)
    result, at, outs = (
        lax.all_to_all(both, axis, split_axis=split_dim, concat_axis=concat_dim, tiled=True),
        0,
        [],
    )
    for a, column in zip(arrays, columns):
        section = result[..., at : at + column.shape[along]]
        outs.append(section.reshape(*section.shape[:along], *a.shape[along:]))
        at += column.shape[along]
    return tuple(outs)


def one_axis_at_a_time(value, axes):
    return functools.reduce(lax.psum, axes, value)


def local_units(values, axes):
    return jnp.sum((values * quantum).astype(jnp.int32), axis=axes)


def split_units(total):
    upper_part = total // limb_base
    return (upper_part, total - upper_part * limb_base)


def join_units(upper_part, lower_part):
    return (upper_part.astype(jnp.float32) * limb_base + lower_part.astype(jnp.float32)) / quantum


def body(ice_flux, ice_frac, ice_mask, ice_area, route, ocean_area, ocean_wet, exponent):
    block_count = route.shape[1]
    field_count = ice_flux.shape[2]
    block_cells = ice_flux.shape[3]
    width_cells = ocean_area.shape[1]
    band_rows = block_cells // width_cells
    tile_count = lax.axis_size("lon")
    amount = ice_area * ice_frac * ice_mask.astype(jnp.float32)
    carried = ice_flux * amount[:, :, None, :]
    source_upper, source_lower = split_units(local_units(carried, (0, 1, 3)))
    block_ids = jnp.arange(block_count, dtype=jnp.int32)
    capacity = max(2, block_count // tile_count)
    targets = route[0]
    target_tile = targets // block_count
    block_row = targets % block_count
    earlier = (target_tile[:, None] == target_tile[None, :]) & (
        block_ids[:, None] > block_ids[None, :]
    )
    ordinal = jnp.sum(earlier.astype(jnp.int32), axis=1)
    slot_index = target_tile * capacity + ordinal
    slot_ids = jnp.arange(tile_count * capacity, dtype=jnp.int32)
    selector = (slot_index[None, :] == slot_ids[:, None]).astype(jnp.float32)
    outgoing = jnp.einsum("qs,sfc->qfc", selector, carried[0], precision=lax.Precision.HIGHEST)
    outgoing_rows = (
        jnp.dot(selector, (block_row + 1).astype(jnp.float32), precision=lax.Precision.HIGHEST)
        - 1.0
    )
    received_rows, arrived_rows = sent_together((outgoing, outgoing_rows), "lon", 0, 0, 1)
    position_mapper = (arrived_rows[None, :] == block_ids.astype(jnp.float32)[:, None]).astype(
        jnp.float32
    )
    block_groups = jnp.einsum(
        "nw,whl->nhl", position_mapper, received_rows, precision=lax.Precision.HIGHEST
    )
    mapped = block_groups.reshape(block_count, field_count, band_rows, width_cells).transpose(
        1, 0, 2, 3
    )
    mapped = mapped.reshape(field_count, block_count * band_rows, width_cells)
    wet_cover = ocean_wet.astype(jnp.float32)
    target_upper, target_lower = split_units(local_units(wet_cover * mapped, (1, 2)))
    wet_upper, wet_lower = split_units(local_units(ocean_area * wet_cover, (0, 1)))
    source_upper, source_lower, target_upper, target_lower, wet_upper, wet_lower = (
        one_axis_at_a_time(source_upper, LAT_LON),
        one_axis_at_a_time(source_lower, LAT_LON),
        one_axis_at_a_time(target_upper, LAT_LON),
        one_axis_at_a_time(target_lower, LAT_LON),
        one_axis_at_a_time(wet_upper, LAT_LON),
        one_axis_at_a_time(wet_lower, LAT_LON),
    )
    source = join_units(source_upper, source_lower)
    target = join_units(target_upper, target_lower)
    wet_area = join_units(wet_upper, wet_lower)
    correction = (source - target) / wet_area
    scaling = jnp.left_shift(jnp.ones_like(exponent), exponent).astype(jnp.float32)
    ocean_flux = (
        wet_cover * scaling[:, None, None] * (mapped / ocean_area + correction[:, None, None])
    )
    return (ocean_flux, source * scaling)


def solution(mesh):
    torus = Mesh(
        mesh.devices.reshape(mesh.shape["member"], 4, 2, mesh.shape["lon"]),
        ("member", "lat_0", "lat_1", "lon"),
    )
    in_specs = (
        P(MEMBER_LAT, "lon", None, None),
        P(MEMBER_LAT, "lon", None),
        P(MEMBER_LAT, "lon", None),
        P(MEMBER_LAT, "lon", None),
        P(MEMBER_LAT, "lon"),
        P(MEMBER_LAT, "lon"),
        P(MEMBER_LAT, "lon"),
        P(),
    )
    out_specs = (P(None, MEMBER_LAT, "lon"), P("member"))
    return jax.shard_map(body, mesh=torus, in_specs=in_specs, out_specs=out_specs, check_vma=False)
```

profile of v0, /device:TPU:24, one launch (start us, length us, event | category | flops | bytes accessed | tf_op | source)
XLA Modules:
  0.0 87.6 jit_solution(4594606004788699273)
XLA Ops:
  0.6 0.0 copy-start.4
  0.6 0.7 and_select_fusion.3
  1.4 0.0 copy-done.4
  1.4 0.8 multiply_bitcast_fusion.1
  2.2 1.0 %multiply_bitcast_fusion = f32[8,512,16]{1,0,2:T(8,128)S(1)} fusion(f32[1,16,8,512]{3,2,1,0:T(8,128)} %param.8, f32[16,512]{1,0:T(8,128)S(1)} %multiply_bitcast_fusion.1), kind=kLoop, calls=%fused_computation.12 | loop fusion | flops 65536 | bytes 557056 | tf_op jit(solution)/shard_map/qs,sfc->qfc/dot_general | solution.py:71
  3.2 0.1 reshape.82
  3.2 0.2 convert_reduce_fusion.3
  3.4 0.1 fusion
  3.6 0.1 concatenate.6
  3.7 0.2 copy.33
  3.9 0.4 fusion.5
  4.4 1.1 %copy.34 = f32[16,2,4097]{2,1,0:T(2,128)} copy(f32[16,2,4097]{2,0,1:T(8,128)S(1)} %pad_maximum_fusion) | data formatting | bytes 1048832 | tf_op jit(solution)/shard_map/concatenate | solution.py:19
  5.4 0.0 copy-start.1
  5.4 15.3 %all-to-all-start = ((f32[16,2,4097]{2,1,0:T(2,128)}), f32[16,2,4097]{2,1,0:T(2,128)S(1)}, u32[]{:S(2)}, u32[]{:S(2)}) async-start(f32[16,2,4097]{2,1,0:T(2,128)} %copy.34), calls=%async_computation | async-start | bytes 1081344 | tf_op jit(solution)/shard_map/all_to_all | solution.py:21
  20.8 0.0 copy-done.1
  20.8 0.0 copy-done.2
  20.8 0.6 convert_reduce_fusion.2
  24.7 0.0 copy-done
  24.7 0.0 copy-start.3
  24.7 0.2 convert_reduce_fusion.1
  24.9 0.5 copy-done.3
  25.4 24.9 %all-to-all-done = f32[16,2,4097]{2,1,0:T(2,128)S(1)} async-done(((f32[16,2,4097]{2,1,0:T(2,128)}), f32[16,2,4097]{2,1,0:T(2,128)S(1)}, u32[]{:S(2)}, u32[]{:S(2)}) %all-to-all-start) | async-done | bytes 524448 | tf_op jit(solution)/shard_map/all_to_all | solution.py:21
  50.3 0.4 all_to_all.7
  50.7 0.1 slice_reduce_fusion
  50.8 0.5 convert_reduce_fusion
  51.4 9.4 %all-reduce.1 = (s32[8]{0:T(128)S(1)}, s32[8]{0:T(128)S(1)}, s32[]{:T(128)}, s32[]{:T(128)}, s32[8]{0:T(128)S(1)}, /*index=5*/s32[8]{0:T(128)S(1)}) all-reduce(s32[8]{0:T(128)S(1)} %get-tuple-element.30, s32[8]{0:T(128)S(1)} %get-tuple-element.31, ...), channel_id=1, replica_groups=mesh['member'=4,'lat_0'=4,'lat_1'=2,'lon'=16] {'lat_0'}, use_global_device_ids=true, to_apply=%region_12.13 | all-reduce | flops 34 | bytes 272 | tf_op jit(solution)/shard_map/psum | solution.py:33
  60.8 2.5 %all-reduce.2 = (s32[8]{0:T(128)S(1)}, s32[8]{0:T(128)S(1)}, s32[]{:T(128)}, s32[]{:T(128)}, s32[8]{0:T(128)S(1)}, /*index=5*/s32[8]{0:T(128)S(1)}) all-reduce(s32[8]{0:T(128)S(1)} %get-tuple-element.16, s32[8]{0:T(128)S(1)} %get-tuple-element.17, ...), channel_id=1, replica_groups=mesh['member'=4,'lat_0'=4,'lat_1'=2,'lon'=16] {'lat_1'}, use_global_device_ids=true, to_apply=%region_13.14 | all-reduce | flops 34 | bytes 272 | tf_op jit(solution)/shard_map/psum | solution.py:33
  63.2 21.6 %all-reduce = (s32[8]{0:T(128)S(1)}, s32[8]{0:T(128)S(1)}, s32[]{:T(128)}, s32[]{:T(128)}, s32[8]{0:T(128)S(1)}, /*index=5*/s32[8]{0:T(128)S(1)}) all-reduce(s32[8]{0:T(128)S(1)} %get-tuple-element.22, s32[8]{0:T(128)S(1)} %get-tuple-element.23, ...), channel_id=1, replica_groups=mesh['member'=4,'lat_0'=4,'lat_1'=2,'lon'=16] {'lon'}, use_global_device_ids=true, to_apply=%region_14.15 | all-reduce | flops 34 | bytes 272 | tf_op jit(solution)/shard_map/psum | solution.py:33
  86.1 0.2 copy.37
  86.3 0.5 fusion.26
  86.8 0.1 fusion.4
  86.9 0.8 copy.39
  (11 shorter events, 0.1 us)
Async XLA Ops:
  0.6 0.7 copy-start.4
  5.4 15.3 %copy-start.1 = (f32[64,128]{1,0:T(8,128)S(1)}, f32[64,128]{1,0:T(8,128)}, u32[]{:S(2)}) copy-start(f32[64,128]{1,0:T(8,128)} %param.13) | copy-start | bytes 98308
  5.4 15.4 %copy-start.2 = (s32[64,128]{1,0:T(8,128)S(1)}, s32[64,128]{1,0:T(8,128)}, u32[]{:S(2)}) copy-start(s32[64,128]{1,0:T(8,128)} %param.14) | copy-start | bytes 98308
  5.4 19.3 %copy-start = (f32[1,16,8,512]{3,2,1,0:T(8,128)S(1)}, f32[1,16,8,512]{3,2,1,0:T(8,128)}, u32[]{:S(2)}) copy-start(f32[1,16,8,512]{3,2,1,0:T(8,128)} %param.8) | copy-start | bytes 786436
  5.4 44.8 %all-to-all-start = ((f32[16,2,4097]{2,1,0:T(2,128)}), f32[16,2,4097]{2,1,0:T(2,128)S(1)}, u32[]{:S(2)}, u32[]{:S(2)}) async-start(f32[16,2,4097]{2,1,0:T(2,128)} %copy.34), calls=%async_computation | async-start | bytes 1081344 | tf_op jit(solution)/shard_map/all_to_all | solution.py:21
  24.7 0.7 copy-start.3
where the time goes:
time: 88.2 us; the launch traced here: 87.6 us
  blocking collectives  33.4 us (38%)
  waiting for transfers between devices  24.9 us (28%)
  starting transfers between devices  15.3 us (17%)
  between operations  5.34 us (6%)
  other arithmetic  4.23 us (5%)
  local copies, waits for them, and re-layouts  3.33 us (4%)
  matrix products  1.09 us (1%)
    psum x3, blocking collectives, one_axis_at_a_time(): return functools.reduce(lax.psum, axes, value)  33.4 us
    all_to_all x1, waiting for transfers between devices, sent_together(): lax.all_to_all(both, axis, split_axis=split_dim, concat_axis=concat_dim,...  24.9 us
    all_to_all x1, starting transfers between devices, sent_together(): lax.all_to_all(both, axis, split_axis=split_dim, concat_axis=concat_dim,...  15.3 us
  transfers between devices with their start and end apart: 1, of which 1 were waited for; matrix products, arithmetic and copies ran while one was open for 1% of the time, Pallas kernels for 0%

commit v1 on v0

v1 whole, which is shorter than its diff:
```python
import jax
import jax.numpy as jnp
from jax import lax
from jax.experimental import pallas as pl
from jax.experimental.pallas import tpu as pltpu
from jax.sharding import Mesh
from jax.sharding import PartitionSpec as P

MEMBER_LAT = ("member", "lat_0", "lat_1")

QUANTUM = 1024.0
LIMB_BITS = 16
LIMB_MASK = 65535
LANES = 128
VMEM_LIMIT = 16 * 1024 * 1024

TARGET_UPPER, TARGET_LOWER, SOURCE_UPPER, SOURCE_LOWER, WET_UPPER, WET_LOWER = 0, 8, 16, 24, 32, 33


def units(values):
    return (values * QUANTUM).astype(jnp.int32)


def spread(per_lane, first_upper, first_lower):
    upper = jnp.sum((per_lane >> LIMB_BITS).astype(jnp.float32), axis=1, keepdims=True)
    lower = jnp.sum((per_lane & LIMB_MASK).astype(jnp.float32), axis=1, keepdims=True)
    lane = lax.broadcasted_iota(jnp.int32, per_lane.shape, 1)
    row = lax.broadcasted_iota(jnp.int32, per_lane.shape, 0)
    placed = jnp.where(lane == row + first_upper, upper, 0.0) + jnp.where(lane == row + first_lower, lower, 0.0)
    return jnp.sum(placed, axis=0, keepdims=True).astype(jnp.int32)


def send_kernel(route, flux, frac, mask, area, ocean_area, ocean_wet, slots, rows, sums, taken):
    blocks = flux.shape[1]
    for i in range(rows.shape[0]):
        rows[i] = blocks
    for tile in range(rows.shape[0] // 2):
        taken[tile] = 0
    amount = area[0] * frac[0] * mask[0].astype(jnp.float32)
    total = jnp.zeros(flux.shape[2:], jnp.int32)
    for b in range(blocks):
        target = route[0, b]
        tile = target // blocks
        slot = 2 * tile + taken[tile]
        taken[tile] = taken[tile] + 1
        rows[slot] = target % blocks
        carried = flux[0, b] * amount[b : b + 1]
        slots[slot] = carried
        total = total + units(carried)
    per_lane = total[:, :LANES]
    for at in range(LANES, total.shape[1], LANES):
        per_lane = per_lane + total[:, at : at + LANES]
    wet = jnp.sum(units(ocean_area[...] * ocean_wet[...].astype(jnp.float32)), axis=0, keepdims=True)
    sums[...] = spread(per_lane, SOURCE_UPPER, SOURCE_LOWER) + spread(wet, WET_UPPER, WET_LOWER)


def place_kernel(lon, rows, received, sent_sums, exponent, ocean_area, ocean_wet, flux, sums, mapped):
    fields = received.shape[1]
    height, width = ocean_area.shape
    stride = mapped.shape[0] // fields
    band = received.shape[2] // width
    me = lon[0]
    for s in range(received.shape[0]):
        row = rows[s // 2, 2 * me + s % 2]
        for r in range(band):
            mapped[pl.ds(row * band + r, fields, stride), :] = received[s, :, r * width : (r + 1) * width]
    cover = ocean_wet[...].astype(jnp.float32)
    per_field = []
    for f in range(fields):
        field = mapped[f * stride : f * stride + height, :]
        per_field.append(jnp.sum(units(cover * field), axis=0, keepdims=True))
        scaling = jnp.left_shift(jnp.int32(1), exponent[f]).astype(jnp.float32)
        flux[f] = cover * scaling * (field / ocean_area[...])
    sums[...] = sent_sums[...] + spread(jnp.concatenate(per_field, axis=0), TARGET_UPPER, TARGET_LOWER)


def joined(sums, upper, lower):
    carry = jnp.right_shift(sums[0, lower], LIMB_BITS)
    high = (sums[0, upper] + carry).astype(jnp.float32)
    low = (sums[0, lower] - carry * (LIMB_MASK + 1)).astype(jnp.float32)
    return (high * float(LIMB_MASK + 1) + low) * (1.0 / QUANTUM)


def correct_kernel(sums, exponent, uncorrected, ocean_wet, flux, source_total):
    fields = uncorrected.shape[0]
    cover = ocean_wet[...].astype(jnp.float32)
    wet_area = jnp.full((1, LANES), joined(sums, WET_UPPER, WET_LOWER), jnp.float32)
    for f in range(fields):
        source = joined(sums, SOURCE_UPPER + f, SOURCE_LOWER + f)
        target = joined(sums, TARGET_UPPER + f, TARGET_LOWER + f)
        scaling = jnp.left_shift(jnp.int32(1), exponent[f]).astype(jnp.float32)
        correction = jnp.full((1, LANES), source - target, jnp.float32) / wet_area
        flux[f] = uncorrected[f] + cover * (correction * scaling)
        source_total[f] = source * scaling


def body(ice_flux, ice_frac, ice_mask, ice_area, route, ocean_area, ocean_wet, exponent):
    blocks, fields, cells = ice_flux.shape[1:]
    height, width = ocean_area.shape
    tiles = lax.axis_size("lon")
    vmem = pl.BlockSpec(memory_space=pltpu.VMEM)
    smem = pl.BlockSpec(memory_space=pltpu.SMEM)
    params = pltpu.CompilerParams(vmem_limit_bytes=VMEM_LIMIT)
    slots, rows, sums = pl.pallas_call(
        send_kernel,
        out_shape=(
            jax.ShapeDtypeStruct((2 * tiles, fields, cells), jnp.float32),
            jax.ShapeDtypeStruct((2 * tiles,), jnp.int32),
            jax.ShapeDtypeStruct((1, LANES), jnp.int32),
        ),
        in_specs=[smem] + [vmem] * 6,
        out_specs=(vmem, smem, vmem),
        scratch_shapes=[pltpu.SMEM((tiles,), jnp.int32)],
        compiler_params=params,
    )(route, ice_flux, ice_frac, ice_mask, ice_area, ocean_area, ocean_wet)
    received = lax.all_to_all(slots, "lon", 0, 0, tiled=True)
    all_rows = lax.all_gather(rows, "lon")
    lon = lax.axis_index("lon").astype(jnp.int32).reshape(1)
    uncorrected, sums = pl.pallas_call(
        place_kernel,
        out_shape=(
            jax.ShapeDtypeStruct((fields, height, width), jnp.float32),
            jax.ShapeDtypeStruct((1, LANES), jnp.int32),
        ),
        in_specs=[smem, smem, vmem, vmem, smem, vmem, vmem],
        out_specs=(vmem, vmem),
        scratch_shapes=[pltpu.VMEM((fields * (height + 8), width), jnp.float32)],
        compiler_params=params,
    )(lon, all_rows, received, sums, exponent, ocean_area, ocean_wet)
    sums = lax.psum(lax.psum(sums, ("lat_0", "lat_1")), "lon")
    return pl.pallas_call(
        correct_kernel,
        out_shape=(
            jax.ShapeDtypeStruct((fields, height, width), jnp.float32),
            jax.ShapeDtypeStruct((fields,), jnp.float32),
        ),
        in_specs=[smem, smem, vmem, vmem],
        out_specs=(vmem, smem),
        compiler_params=params,
    )(sums, exponent, uncorrected, ocean_wet)


def solution(mesh):
    torus = Mesh(
        mesh.devices.reshape(mesh.shape["member"], 4, 2, mesh.shape["lon"]),
        ("member", "lat_0", "lat_1", "lon"),
    )
    in_specs = (
        P(MEMBER_LAT, "lon", None, None),
        P(MEMBER_LAT, "lon", None),
        P(MEMBER_LAT, "lon", None),
        P(MEMBER_LAT, "lon", None),
        P(MEMBER_LAT, "lon"),
        P(MEMBER_LAT, "lon"),
        P(MEMBER_LAT, "lon"),
        P(),
    )
    out_specs = (P(None, MEMBER_LAT, "lon"), P("member"))
    return jax.shard_map(body, mesh=torus, in_specs=in_specs, out_specs=out_specs, check_vma=False)
```

time: 88.2 us -> 93.4 us (1.059)
  blocking collectives: 33.4 us -> 64.7 us
  waiting for transfers between devices: 24.9 us -> 0.01 us
  local copies, waits for them, and re-layouts: 3.33 us -> 7.63 us
  other arithmetic: 4.23 us -> 0 us
  between operations: 5.34 us -> 1.36 us
  Pallas kernels: 0 us -> 3.74 us
  matrix products: 1.09 us -> 0 us
    unnamed x0 -> x1, blocking collectives: none -> 37.4 us
    all_to_all x1, waiting for transfers between devices: 24.9 us -> 0.01 us  [body(): received = lax.all_to_all(slots, 'lon', 0, 0, tiled=True)]
    unnamed x11 -> x23, local copies, waits for them, and re-layouts: 1.23 us -> 7.56 us
    psum x3 -> x2, blocking collectives: 33.4 us -> 27.3 us  [body(): sums = lax.psum(lax.psum(sums, ('lat_0', 'lat_1')), 'lon')]
    pallas_call x0 -> x3, Pallas kernels: none -> 3.74 us  [the longest x1 1.51 us: body(): pl.pallas_call(send_kernel, out_shape=(jax.ShapeDtypeStruct((2 * tiles, f...]
    mul x3 -> x0, other arithmetic: 1.42 us -> none  [the longest x1 0.8 us: body(): carried = ice_flux * amount[:, :, None, :]]
    concatenate x3 -> x0, local copies, waits for them, and re-layouts: 1.37 us -> none  [sent_together(): both = jnp.concatenate(columns, axis=along)]
    dot_general x3 -> x0, matrix products: 1.09 us -> none  [the longest x1 0.53 us: body(): jnp.einsum('nw,whl->nhl', position_mapper, received_rows, precision=lax.P...]
  transfers between devices with their start and end apart: 1 -> 1, of which waited for: 1 -> 0; matrix products, arithmetic and copies ran while one was open for 1% -> 2% of each run, Pallas kernels for 0% -> 0%
where the time goes in v1:
time: 93.4 us; the launch traced here: 92.6 us
  blocking collectives  64.7 us (69%)
  starting transfers between devices  15.2 us (16%)
  local copies, waits for them, and re-layouts  7.63 us (8%)
  Pallas kernels  3.74 us (4%)
  between operations  1.36 us (1%)
    unnamed x1, blocking collectives  37.4 us
    psum x2, blocking collectives, body(): sums = lax.psum(lax.psum(sums, ('lat_0', 'lat_1')), 'lon')  27.3 us
    all_to_all x1, starting transfers between devices, body(): received = lax.all_to_all(slots, 'lon', 0, 0, tiled=True)  15.2 us
    unnamed x23, local copies, waits for them, and re-layouts  7.56 us
  transfers between devices with their start and end apart: 1, of which 0 were waited for; matrix products, arithmetic and copies ran while one was open for 2% of the time, Pallas kernels for 0%

profile of v1, /device:TPU:24, one launch (start us, length us, event | category | flops | bytes accessed | tf_op | source)
XLA Modules:
  0.0 92.6 jit_solution(14202986465003092679)
XLA Ops:
  0.6 0.0 copy-start
  0.6 0.7 copy-done
  1.4 0.0 copy-start.2
  1.4 0.9 %copy-done.2 = f32[1,16,8,512]{3,2,1,0:T(8,128)S(1)} copy-done((f32[1,16,8,512]{3,2,1,0:T(8,128)S(1)}, f32[1,16,8,512]{3,2,1,0:T(8,128)}, u32[]{:S(2)}) %copy-start.2) | copy-done | bytes 262168
  2.3 0.0 copy-start.3
  2.3 0.8 copy-done.3
  3.1 0.0 copy-start.5
  3.1 0.8 copy-done.5
  3.9 0.0 copy-start.6
  3.9 0.8 copy-done.6
  4.6 0.0 copy-start.7
  4.6 0.8 copy-done.7
  5.4 0.0 copy-start.9
  5.4 0.7 copy-done.9
  6.0 1.5 %shard_map.95 = (f32[32,8,512]{2,1,0:T(8,128)}, s32[32]{0:T(128)S(1)}, s32[1,128]{1,0:T(1,128)S(1)}) custom-call(s32[1,16]{1,0:T(1,128)S(1)} %copy-done.9, f32[1,16,8,512]{3,2,1,0:T(8,128)S(1)} %copy-done.2, f32[1,16,512]{2,1,0:T(8,128)S(1)} %copy-done.5, s32[1,16,512]{2,1,0:T(8,128)S(1)} %copy-done.6, f32[1,16,512]{2,1,0:T(8,128)S(1)} %copy-done.7, ...), custom_call_target="tpu_custom_call" | custom-call | tf_op jit(solution)/shard_map/pallas_call | solution.py:104
  7.5 0.0 copy-start.4
  7.6 15.2 %all-to-all-start = ((f32[32,8,512]{2,1,0:T(8,128)}), f32[32,8,512]{2,1,0:T(8,128)S(1)}, u32[]{:S(2)}, u32[]{:S(2)}) async-start(f32[32,8,512]{2,1,0:T(8,128)} %get-tuple-element.8), calls=%async_computation | async-start | bytes 1048576 | tf_op jit(solution)/shard_map/all_to_all | solution.py:116
  22.8 0.0 copy-start.1
  22.8 1.3 %dynamic-slice = u32[1]{0:T(128)} dynamic-slice(u32[512]{0:T(512)} %constant.11, u32[]{:T(128)S(6)} %add.4), dynamic_slice_sizes={1} | dynamic-slice | bytes 12
  24.7 0.2 dynamic-update-slice
  25.0 37.4 %all-reduce = s32[512]{0:T(512)S(1)} all-reduce(s32[512]{0:T(512)S(1)} %dynamic-update-slice), channel_id=2, replica_groups=mesh['member'=4,'lat_0'=4,'lat_1'=2,'lon'=16] {'lon'}, use_global_device_ids=true, to_apply=%add | all-reduce | flops 512 | bytes 4096
  62.3 0.1 reshape.8.rows
  62.4 0.0 all-to-all-done.received
  62.4 0.0 copy-start.8
  62.4 0.0 copy-done.4
  62.4 0.0 copy-done.1
  62.4 0.6 copy-done.8
  63.1 0.9 shard_map.96
  64.0 9.2 %psum.14 = s32[1,128]{1,0:T(1,128)S(1)} all-reduce(s32[1,128]{1,0:T(1,128)S(1)} %get-tuple-element.10), channel_id=1, replica_groups=mesh['member'=4,'lat_0'=4,'lat_1'=2,'lon'=16] {'lat_0','lat_1'}, use_global_device_ids=true, to_apply=%region_0.0 | all-reduce | flops 128 | bytes 1024 | tf_op jit(solution)/shard_map/psum | solution.py:130
  73.2 18.1 %psum.15.sums = s32[1,128]{1,0:T(1,128)S(1)} all-reduce(s32[1,128]{1,0:T(1,128)S(1)} %psum.14), channel_id=1, replica_groups=mesh['member'=4,'lat_0'=4,'lat_1'=2,'lon'=16] {'lon'}, use_global_device_ids=true, to_apply=%region_1.0 | all-reduce | flops 128 | bytes 1024 | tf_op jit(solution)/shard_map/psum | solution.py:130
  91.3 1.3 %shard_map.97 = (f32[8,64,128]{2,1,0:T(8,128)}, f32[8]{0:T(128)}) custom-call(s32[1,128]{1,0:T(1,128)S(1)} %psum.15.sums, s32[8]{0:T(128)S(1)} %copy-done.8, f32[8,64,128]{2,1,0:T(8,128)S(1)} %get-tuple-element.11.uncorrected, s32[64,128]{1,0:T(8,128)S(1)} %copy-done.1), custom_call_target="tpu_custom_call" | custom-call | tf_op jit(solution)/shard_map/pallas_call | solution.py:131
  (1 shorter events, 0.0 us)
Async XLA Ops:
  0.6 0.8 copy-start
  1.4 0.9 %copy-start.2 = (f32[1,16,8,512]{3,2,1,0:T(8,128)S(1)}, f32[1,16,8,512]{3,2,1,0:T(8,128)}, u32[]{:S(2)}) copy-start(f32[1,16,8,512]{3,2,1,0:T(8,128)} %flux.1) | copy-start | bytes 786436
  2.3 0.8 copy-start.3
  3.1 0.8 copy-start.5
  3.9 0.8 copy-start.6
  4.6 0.8 copy-start.7
  5.4 0.7 copy-start.9
  7.5 54.9 %copy-start.4 = (f32[64,128]{1,0:T(8,128)S(1)}, f32[64,128]{1,0:T(8,128)}, u32[]{:S(2)}) copy-start(f32[64,128]{1,0:T(8,128)} %ocean_area.3) | copy-start | bytes 98308
  7.6 54.8 %all-to-all-start = ((f32[32,8,512]{2,1,0:T(8,128)}), f32[32,8,512]{2,1,0:T(8,128)S(1)}, u32[]{:S(2)}, u32[]{:S(2)}) async-start(f32[32,8,512]{2,1,0:T(8,128)} %get-tuple-element.8), calls=%async_computation | async-start | bytes 1048576 | tf_op jit(solution)/shard_map/all_to_all | solution.py:116
  22.8 39.6 %copy-start.1 = (s32[64,128]{1,0:T(8,128)S(1)}, s32[64,128]{1,0:T(8,128)}, u32[]{:S(2)}) copy-start(s32[64,128]{1,0:T(8,128)} %ocean_wet.5) | copy-start | bytes 98308
  62.4 0.7 copy-start.8

commit v2 on v1

v2 whole, which is shorter than its diff:
```python
import jax
import jax.numpy as jnp
from jax import lax
from jax.experimental import pallas as pl
from jax.experimental.pallas import tpu as pltpu
from jax.sharding import Mesh
from jax.sharding import PartitionSpec as P

MEMBER_LAT = ("member", "lat_0", "lat_1")
LAT = ("lat_0", "lat_1")

QUANTUM = 1024.0
LIMB_BITS = 16
LIMB_MASK = 65535
LANES = 128
VMEM_LIMIT = 16 * 1024 * 1024
SEND_VMEM_LIMIT = 62 * 1024 * 1024
PIECES = 4

TARGET, SOURCE, WET = 0, 16, 32
LOWER = 8


def units(values):
    return (values * QUANTUM).astype(jnp.int32)


def spread(per_lane, first):
    upper = jnp.sum((per_lane >> LIMB_BITS).astype(jnp.float32), axis=1, keepdims=True)
    lower = jnp.sum((per_lane & LIMB_MASK).astype(jnp.float32), axis=1, keepdims=True)
    lane = lax.broadcasted_iota(jnp.int32, per_lane.shape, 1)
    row = lax.broadcasted_iota(jnp.int32, per_lane.shape, 0)
    placed = jnp.where(lane == row + first, upper, 0.0) + jnp.where(lane == row + first + LOWER, lower, 0.0)
    return jnp.sum(placed, axis=0, keepdims=True).astype(jnp.int32)


def send_kernel(route, flux, frac, mask, area, chunks, route_s, flux_v, frac_v, mask_v, area_v, taken, sems):
    blocks, fields, cells = flux_v.shape
    tiles = chunks.shape[0]
    band = cells // LANES
    copies = [
        pltpu.make_async_copy(route.at[0], route_s, sems.at[0]),
        pltpu.make_async_copy(frac.at[0], frac_v, sems.at[1]),
        pltpu.make_async_copy(mask.at[0], mask_v, sems.at[2]),
        pltpu.make_async_copy(area.at[0], area_v, sems.at[3]),
    ]
    piece = blocks // PIECES
    for p in range(PIECES):
        part = pl.ds(p * piece, piece)
        copies.append(pltpu.make_async_copy(flux.at[0, part], flux_v.at[part], sems.at[4 + p]))
    for copy in copies:
        copy.start()
    for tile in range(tiles):
        taken[tile] = 0
    nobody = jnp.full((8, LANES), float(blocks), jnp.float32)
    for tile in range(tiles):
        chunks[tile, 2 * band * fields :, :] = nobody
    for copy in copies[:4]:
        copy.wait()
    amount = area_v[...] * frac_v[...] * mask_v[...].astype(jnp.float32)
    for b in range(blocks):
        if b % piece == 0:
            copies[4 + b // piece].wait()
        target = route_s[b]
        tile = target // blocks
        order = taken[tile]
        taken[tile] = order + 1
        carried = flux_v[b] * amount[b : b + 1]
        first = pl.multiple_of(order * (band * fields), band * fields)
        for r in range(band):
            chunks[tile, pl.ds(first + r * fields, fields), :] = carried[:, r * LANES : (r + 1) * LANES]
        row = jnp.full((1, LANES), target % blocks, jnp.int32).astype(jnp.float32)
        chunks[tile, pl.ds(2 * band * fields + order, 1), :] = row


def beside_kernel(exponent, flux, frac, mask, area, ocean_area, ocean_wet, sums, scaling):
    amount = area[0] * frac[0] * mask[0].astype(jnp.float32)
    total = jnp.zeros(flux.shape[2:], jnp.int32)
    for b in range(flux.shape[1]):
        total = total + units(flux[0, b] * amount[b : b + 1])
    per_lane = total[:, :LANES]
    for at in range(LANES, total.shape[1], LANES):
        per_lane = per_lane + total[:, at : at + LANES]
    wet = jnp.sum(units(ocean_area[...] * ocean_wet[...].astype(jnp.float32)), axis=0, keepdims=True)
    sums[...] = spread(per_lane, SOURCE) + spread(wet, WET)
    lane = lax.broadcasted_iota(jnp.int32, (1, LANES), 1)
    scales = jnp.ones((1, LANES), jnp.int32)
    for f in range(flux.shape[2]):
        scales = jnp.where(lane == f, jnp.left_shift(jnp.int32(1), exponent[f]), scales)
    scaling[...] = scales.astype(jnp.float32)


def place_kernel(received, sent_sums, ocean_area, ocean_wet, quotient, sums, mapped):
    fields, height, width = quotient.shape
    stride = mapped.shape[0] // fields
    band = (received.shape[1] - 8) // (2 * fields)
    for s in range(received.shape[0]):
        for order in range(2):
            at = (2 * s + order) * band * fields
            row = received[s, 2 * band * fields + order, 0].astype(jnp.int32)
            for r in range(band):
                first = (order * band + r) * fields
                mapped[pl.ds(row * band + r, fields, stride), :] = received[s, first : first + fields, :]
    cover = ocean_wet[...].astype(jnp.float32)
    per_field = []
    for f in range(fields):
        field = mapped[f * stride : f * stride + height, :]
        per_field.append(jnp.sum(units(cover * field), axis=0, keepdims=True))
        quotient[f] = field / ocean_area[...]
    sums[...] = sent_sums[...] + spread(jnp.concatenate(per_field, axis=0), TARGET)


def correct_kernel(sums, scaling, quotient, ocean_wet, flux, source_total):
    fields = quotient.shape[0]
    upper = jnp.broadcast_to(sums[...], (8, LANES))
    lower = pltpu.roll(upper, LANES - LOWER, 1)
    upper = (upper + (lower >> LIMB_BITS)).astype(jnp.float32)
    integral = (upper * float(LIMB_MASK + 1) + (lower & LIMB_MASK).astype(jnp.float32)) * (1.0 / QUANTUM)
    source = pltpu.roll(integral, LANES - (SOURCE - TARGET), 1)
    lane = lax.broadcasted_iota(jnp.int32, (8, LANES), 1)
    row = lax.broadcasted_iota(jnp.int32, (8, LANES), 0)
    wet_area = jnp.sum(jnp.where(lane == WET, integral, 0.0), axis=1, keepdims=True)
    correction = (source - integral) / wet_area
    scales = jnp.broadcast_to(scaling[...], (8, LANES))
    per_field = jnp.sum(jnp.where(lane == row, correction, 0.0), axis=1, keepdims=True)
    scale = jnp.sum(jnp.where(lane == row, scales, 0.0), axis=1, keepdims=True)
    cover = ocean_wet[...].astype(jnp.float32)
    for f in range(fields):
        flux[f] = cover * scale[f : f + 1] * (quotient[f] + per_field[f : f + 1])
    source_total[...] = (source * scales)[0, :fields]


def body(ice_flux, ice_frac, ice_mask, ice_area, route, ocean_area, ocean_wet, exponent):
    blocks, fields, cells = ice_flux.shape[1:]
    height, width = ocean_area.shape
    tiles = lax.axis_size("lon")
    chunk_rows = 2 * fields * cells // LANES + 8
    vmem = pl.BlockSpec(memory_space=pltpu.VMEM)
    smem = pl.BlockSpec(memory_space=pltpu.SMEM)
    hbm = pl.BlockSpec(memory_space=pltpu.HBM)
    params = pltpu.CompilerParams(vmem_limit_bytes=VMEM_LIMIT)
    chunks = pl.pallas_call(
        send_kernel,
        out_shape=jax.ShapeDtypeStruct((tiles, chunk_rows, LANES), jnp.float32),
        in_specs=[hbm] * 5,
        out_specs=vmem,
        scratch_shapes=[
            pltpu.SMEM((blocks,), jnp.int32),
            pltpu.VMEM((blocks, fields, cells), jnp.float32),
            pltpu.VMEM((blocks, cells), jnp.float32),
            pltpu.VMEM((blocks, cells), jnp.int32),
            pltpu.VMEM((blocks, cells), jnp.float32),
            pltpu.SMEM((tiles,), jnp.int32),
            pltpu.SemaphoreType.DMA((4 + PIECES,)),
        ],
        compiler_params=pltpu.CompilerParams(vmem_limit_bytes=SEND_VMEM_LIMIT),
    )(route, ice_flux, ice_frac, ice_mask, ice_area)
    received = lax.all_to_all(chunks, "lon", 0, 0, tiled=True)
    sums, scaling = pl.pallas_call(
        beside_kernel,
        out_shape=(
            jax.ShapeDtypeStruct((1, LANES), jnp.int32),
            jax.ShapeDtypeStruct((1, LANES), jnp.float32),
        ),
        in_specs=[smem] + [vmem] * 6,
        out_specs=(vmem, vmem),
        compiler_params=params,
    )(exponent, ice_flux, ice_frac, ice_mask, ice_area, ocean_area, ocean_wet)
    quotient, sums = pl.pallas_call(
        place_kernel,
        out_shape=(
            jax.ShapeDtypeStruct((fields, height, width), jnp.float32),
            jax.ShapeDtypeStruct((1, LANES), jnp.int32),
        ),
        in_specs=[vmem] * 4,
        out_specs=(vmem, vmem),
        scratch_shapes=[pltpu.VMEM((fields * (height + 8), width), jnp.float32)],
        compiler_params=params,
    )(received, sums, ocean_area, ocean_wet)
    sums = lax.psum(lax.psum(sums, LAT), "lon")
    return pl.pallas_call(
        correct_kernel,
        out_shape=(
            jax.ShapeDtypeStruct((fields, height, width), jnp.float32),
            jax.ShapeDtypeStruct((fields,), jnp.float32),
        ),
        in_specs=[vmem] * 4,
        out_specs=(vmem, vmem),
        compiler_params=params,
    )(sums, scaling, quotient, ocean_wet)


def solution(mesh):
    torus = Mesh(
        mesh.devices.reshape(mesh.shape["member"], 4, 2, mesh.shape["lon"]),
        ("member", "lat_0", "lat_1", "lon"),
    )
    in_specs = (
        P(MEMBER_LAT, "lon", None, None),
        P(MEMBER_LAT, "lon", None),
        P(MEMBER_LAT, "lon", None),
        P(MEMBER_LAT, "lon", None),
        P(MEMBER_LAT, "lon"),
        P(MEMBER_LAT, "lon"),
        P(MEMBER_LAT, "lon"),
        P(),
    )
    out_specs = (P(None, MEMBER_LAT, "lon"), P("member"))
    return jax.shard_map(body, mesh=torus, in_specs=in_specs, out_specs=out_specs, check_vma=False)
```

time: 93.4 us -> 81.3 us (0.87)
  blocking collectives: 64.7 us -> 30.9 us
  waiting for transfers between devices: 0.01 us -> 30 us
  local copies, waits for them, and re-layouts: 7.63 us -> 0.04 us
    unnamed x1 -> x0, blocking collectives: 37.4 us -> none
    all_to_all x1, waiting for transfers between devices: 0.01 us -> 30 us  [body(): received = lax.all_to_all(chunks, 'lon', 0, 0, tiled=True)]
    unnamed x23 -> x14, local copies, waits for them, and re-layouts: 7.56 us -> 0.04 us
    psum x2, blocking collectives: 27.3 us -> 30.9 us  [body(): sums = lax.psum(lax.psum(sums, LAT), 'lon')]
    pallas_call x1 -> x2, Pallas kernels: 1.51 us -> 2.63 us  [the longest x1 1.93 us: body(): pl.pallas_call(send_kernel, out_shape=jax.ShapeDtypeStruct((tiles, chunk_...]
  transfers between devices with their start and end apart: 1 -> 1, of which waited for: 0 -> 1; matrix products, arithmetic and copies ran while one was open for 2% -> 0% of each run, Pallas kernels for 0% -> 1%
where the time goes in v2:
time: 81.3 us; the launch traced here: 81 us
  blocking collectives  30.9 us (38%)
  waiting for transfers between devices  30 us (37%)
  starting transfers between devices  15.3 us (19%)
  Pallas kernels  3.87 us (5%)
    psum x2, blocking collectives, body(): sums = lax.psum(lax.psum(sums, LAT), 'lon')  30.9 us
    all_to_all x1, waiting for transfers between devices, body(): received = lax.all_to_all(chunks, 'lon', 0, 0, tiled=True)  30 us
    all_to_all x1, starting transfers between devices, body(): received = lax.all_to_all(chunks, 'lon', 0, 0, tiled=True)  15.3 us
    pallas_call x1, Pallas kernels, body(): pl.pallas_call(send_kernel, out_shape=jax.ShapeDtypeStruct((tiles, chunk_...  1.93 us
  transfers between devices with their start and end apart: 1, of which 1 were waited for; matrix products, arithmetic and copies ran while one was open for 0% of the time, Pallas kernels for 1%

profile of v2, /device:TPU:24, one launch (start us, length us, event | category | flops | bytes accessed | tf_op | source)
XLA Modules:
  0.0 81.0 jit_solution(385410235610806167)
XLA Ops:
  0.6 1.9 %shard_map.95 = f32[16,72,128]{2,1,0:T(8,128)} custom-call(s32[1,16]{1,0:T(1,128)} %route.1, f32[1,16,8,512]{3,2,1,0:T(8,128)} %flux.3, f32[1,16,512]{2,1,0:T(8,128)} %frac.3, s32[1,16,512]{2,1,0:T(8,128)} %mask.3, f32[1,16,512]{2,1,0:T(8,128)} %area.3), custom_call_target="tpu_custom_call" | custom-call | tf_op jit(solution)/shard_map/pallas_call | solution.py:142
  2.6 0.0 copy-start
  2.6 0.0 copy-start.1
  2.6 0.0 copy-start.2
  2.6 0.0 copy-start.3
  2.6 0.0 copy-start.4
  2.6 0.0 copy-start.5
  2.6 0.0 copy-start.6
  2.7 15.3 %all-to-all-start = ((f32[16,72,128]{2,1,0:T(8,128)}), f32[16,72,128]{2,1,0:T(8,128)S(1)}, u32[]{:S(2)}, u32[]{:S(2)}) async-start(f32[16,72,128]{2,1,0:T(8,128)} %shard_map.95), calls=%async_computation | async-start | bytes 1179648 | tf_op jit(solution)/shard_map/all_to_all | solution.py:158
  18.0 0.0 copy-done
  18.0 0.0 copy-done.1
  18.0 0.0 copy-done.2
  18.0 0.0 copy-done.3
  18.0 0.0 copy-done.4
  18.0 0.0 copy-done.5
  18.1 0.0 copy-done.6
  18.1 0.7 shard_map.96
  18.8 30.0 %all-to-all-done.received = f32[16,72,128]{2,1,0:T(8,128)S(1)} async-done(((f32[16,72,128]{2,1,0:T(8,128)}), f32[16,72,128]{2,1,0:T(8,128)S(1)}, u32[]{:S(2)}, u32[]{:S(2)}) %all-to-all-start) | async-done | bytes 589856 | tf_op jit(solution)/shard_map/all_to_all | solution.py:158
  48.8 0.3 shard_map.97
  49.1 9.2 %psum.14 = s32[1,128]{1,0:T(1,128)S(1)} all-reduce(s32[1,128]{1,0:T(1,128)S(1)} %get-tuple-element.7), channel_id=1, replica_groups=mesh['member'=4,'lat_0'=4,'lat_1'=2,'lon'=16] {'lat_0','lat_1'}, use_global_device_ids=true, to_apply=%region_0.0 | all-reduce | flops 128 | bytes 1024 | tf_op jit(solution)/shard_map/psum | solution.py:180
  58.3 21.7 %psum.15.sums = s32[1,128]{1,0:T(1,128)S(1)} all-reduce(s32[1,128]{1,0:T(1,128)S(1)} %psum.14), channel_id=1, replica_groups=mesh['member'=4,'lat_0'=4,'lat_1'=2,'lon'=16] {'lon'}, use_global_device_ids=true, to_apply=%region_1.0 | all-reduce | flops 128 | bytes 1024 | tf_op jit(solution)/shard_map/psum | solution.py:180
  80.0 1.0 %shard_map.98 = (f32[8,64,128]{2,1,0:T(8,128)}, f32[8]{0:T(128)}) custom-call(s32[1,128]{1,0:T(1,128)S(1)} %psum.15.sums, f32[1,128]{1,0:T(1,128)S(1)} %get-tuple-element.8.scaling, f32[8,64,128]{2,1,0:T(8,128)S(1)} %get-tuple-element.9.quotient, s32[64,128]{1,0:T(8,128)S(1)} %copy-done.1), custom_call_target="tpu_custom_call" | custom-call | tf_op jit(solution)/shard_map/pallas_call | solution.py:181
Async XLA Ops:
  2.6 15.4 %copy-start = (f32[1,16,8,512]{3,2,1,0:T(8,128)S(1)}, f32[1,16,8,512]{3,2,1,0:T(8,128)}, u32[]{:S(2)}) copy-start(f32[1,16,8,512]{3,2,1,0:T(8,128)} %flux.3) | copy-start | bytes 786436
  2.6 15.4 %copy-start.1 = (s32[64,128]{1,0:T(8,128)S(1)}, s32[64,128]{1,0:T(8,128)}, u32[]{:S(2)}) copy-start(s32[64,128]{1,0:T(8,128)} %ocean_wet.5) | copy-start | bytes 98308
  2.6 15.4 %copy-start.2 = (f32[1,16,512]{2,1,0:T(8,128)S(1)}, f32[1,16,512]{2,1,0:T(8,128)}, u32[]{:S(2)}) copy-start(f32[1,16,512]{2,1,0:T(8,128)} %frac.3) | copy-start | bytes 98308
  2.6 15.4 %copy-start.3 = (s32[1,16,512]{2,1,0:T(8,128)S(1)}, s32[1,16,512]{2,1,0:T(8,128)}, u32[]{:S(2)}) copy-start(s32[1,16,512]{2,1,0:T(8,128)} %mask.3) | copy-start | bytes 98308
  2.6 15.4 %copy-start.4 = (f32[1,16,512]{2,1,0:T(8,128)S(1)}, f32[1,16,512]{2,1,0:T(8,128)}, u32[]{:S(2)}) copy-start(f32[1,16,512]{2,1,0:T(8,128)} %area.3) | copy-start | bytes 98308
  2.6 15.4 %copy-start.5 = (f32[64,128]{1,0:T(8,128)S(1)}, f32[64,128]{1,0:T(8,128)}, u32[]{:S(2)}) copy-start(f32[64,128]{1,0:T(8,128)} %ocean_area.3) | copy-start | bytes 98308
  2.6 15.4 %copy-start.6 = (s32[8]{0:T(128)S(1)}, s32[8]{0:T(128)}, u32[]{:S(2)}) copy-start(s32[8]{0:T(128)} %exponent.1) | copy-start | bytes 100
  2.7 46.2 %all-to-all-start = ((f32[16,72,128]{2,1,0:T(8,128)}), f32[16,72,128]{2,1,0:T(8,128)S(1)}, u32[]{:S(2)}, u32[]{:S(2)}) async-start(f32[16,72,128]{2,1,0:T(8,128)} %shard_map.95), calls=%async_computation | async-start | bytes 1179648 | tf_op jit(solution)/shard_map/all_to_all | solution.py:158

commit v3 on v2

--- a/solution.py
+++ b/solution.py
@@ -34,43 +34,55 @@
     return jnp.sum(placed, axis=0, keepdims=True).astype(jnp.int32)
 
 
-def send_kernel(route, flux, frac, mask, area, chunks, route_s, flux_v, frac_v, mask_v, area_v, taken, sems):
+def send_kernel(route, flux, frac, mask, area, chunks, route_s, flux_v, frac_v, mask_v, area_v, staged, rows, taken, place, in_sems, out_sems):
     blocks, fields, cells = flux_v.shape
     tiles = chunks.shape[0]
     band = cells // LANES
-    copies = [
-        pltpu.make_async_copy(route.at[0], route_s, sems.at[0]),
-        pltpu.make_async_copy(frac.at[0], frac_v, sems.at[1]),
-        pltpu.make_async_copy(mask.at[0], mask_v, sems.at[2]),
-        pltpu.make_async_copy(area.at[0], area_v, sems.at[3]),
-    ]
+    block_rows = band * fields
+    route_in = pltpu.make_async_copy(route.at[0], route_s, in_sems.at[0])
+    frac_in = pltpu.make_async_copy(frac.at[0], frac_v, in_sems.at[1])
+    mask_in = pltpu.make_async_copy(mask.at[0], mask_v, in_sems.at[2])
+    area_in = pltpu.make_async_copy(area.at[0], area_v, in_sems.at[3])
     piece = blocks // PIECES
+    flux_in = []
     for p in range(PIECES):
         part = pl.ds(p * piece, piece)
-        copies.append(pltpu.make_async_copy(flux.at[0, part], flux_v.at[part], sems.at[4 + p]))
-    for copy in copies:
+        flux_in.append(pltpu.make_async_copy(flux.at[0, part], flux_v.at[part], in_sems.at[4 + p]))
+    for copy in [route_in, frac_in, mask_in, area_in] + flux_in:
         copy.start()
     for tile in range(tiles):
         taken[tile] = 0
     nobody = jnp.full((8, LANES), float(blocks), jnp.float32)
     for tile in range(tiles):
-        chunks[tile, 2 * band * fields :, :] = nobody
-    for copy in copies[:4]:
-        copy.wait()
-    amount = area_v[...] * frac_v[...] * mask_v[...].astype(jnp.float32)
+        rows[tile] = nobody
+    route_in.wait()
     for b in range(blocks):
-        if b % piece == 0:
-            copies[4 + b // piece].wait()
         target = route_s[b]
         tile = target // blocks
         order = taken[tile]
         taken[tile] = order + 1
+        place[b] = 2 * tile + order
+        rows[tile, pl.ds(order, 1), :] = jnp.full((1, LANES), target % blocks, jnp.int32).astype(jnp.float32)
+    rows_out = pltpu.make_async_copy(rows, chunks.at[:, pl.ds(2 * block_rows, 8)], out_sems.at[blocks])
+    rows_out.start()
+    frac_in.wait()
+    mask_in.wait()
+    area_in.wait()
+    amount = area_v[...] * frac_v[...] * mask_v[...].astype(jnp.float32)
+    blocks_out = []
+    for b in range(blocks):
+        if b % piece == 0:
+            flux_in[b // piece].wait()
         carried = flux_v[b] * amount[b : b + 1]
-        first = pl.multiple_of(order * (band * fields), band * fields)
         for r in range(band):
-            chunks[tile, pl.ds(first + r * fields, fields), :] = carried[:, r * LANES : (r + 1) * LANES]
-        row = jnp.full((1, LANES), target % blocks, jnp.int32).astype(jnp.float32)
-        chunks[tile, pl.ds(2 * band * fields + order, 1), :] = row
+            staged[b, r * fields : (r + 1) * fields, :] = carried[:, r * LANES : (r + 1) * LANES]
+        first = pl.multiple_of((place[b] % 2) * block_rows, block_rows)
+        to = chunks.at[place[b] // 2, pl.ds(first, block_rows)]
+        blocks_out.append(pltpu.make_async_copy(staged.at[b], to, out_sems.at[b]))
+        blocks_out[b].start()
+    rows_out.wait()
+    for copy in blocks_out:
+        copy.wait()
 
 
 def beside_kernel(exponent, flux, frac, mask, area, ocean_area, ocean_wet, sums, scaling):
@@ -143,15 +155,19 @@
         send_kernel,
         out_shape=jax.ShapeDtypeStruct((tiles, chunk_rows, LANES), jnp.float32),
         in_specs=[hbm] * 5,
-        out_specs=vmem,
+        out_specs=hbm,
         scratch_shapes=[
             pltpu.SMEM((blocks,), jnp.int32),
             pltpu.VMEM((blocks, fields, cells), jnp.float32),
             pltpu.VMEM((blocks, cells), jnp.float32),
             pltpu.VMEM((blocks, cells), jnp.int32),
             pltpu.VMEM((blocks, cells), jnp.float32),
+            pltpu.VMEM((blocks, fields * cells // LANES, LANES), jnp.float32),
+            pltpu.VMEM((tiles, 8, LANES), jnp.float32),
             pltpu.SMEM((tiles,), jnp.int32),
+            pltpu.SMEM((blocks,), jnp.int32),
             pltpu.SemaphoreType.DMA((4 + PIECES,)),
+            pltpu.SemaphoreType.DMA((blocks + 1,)),
         ],
         compiler_params=pltpu.CompilerParams(vmem_limit_bytes=SEND_VMEM_LIMIT),
     )(route, ice_flux, ice_frac, ice_mask, ice_area)
@@ -177,7 +193,7 @@
         scratch_shapes=[pltpu.VMEM((fields * (height + 8), width), jnp.float32)],
         compiler_params=params,
     )(received, sums, ocean_area, ocean_wet)
-    sums = lax.psum(lax.psum(sums, LAT), "lon")
+    sums = lax.psum(sums, LAT + ("lon",))
     return pl.pallas_call(
         correct_kernel,
         out_shape=(

time: 81.3 us -> 79.9 us (0.983)
  blocking collectives: 30.9 us -> 29.2 us
    psum x2 -> x1, blocking collectives: 30.9 us -> 29.2 us  [body(): sums = lax.psum(sums, LAT + ('lon',))]
where the time goes in v3:
time: 79.9 us; the launch traced here: 79.2 us
  waiting for transfers between devices  30 us (38%)
  blocking collectives  29.2 us (37%)
  starting transfers between devices  15.3 us (19%)
  Pallas kernels  3.8 us (5%)
    all_to_all x1, waiting for transfers between devices, body(): received = lax.all_to_all(chunks, 'lon', 0, 0, tiled=True)  30 us
    psum x1, blocking collectives, body(): sums = lax.psum(sums, LAT + ('lon',))  29.2 us
    all_to_all x1, starting transfers between devices, body(): received = lax.all_to_all(chunks, 'lon', 0, 0, tiled=True)  15.3 us
    pallas_call x1, Pallas kernels, body(): pl.pallas_call(send_kernel, out_shape=jax.ShapeDtypeStruct((tiles, chunk_...  1.86 us
  transfers between devices with their start and end apart: 1, of which 1 were waited for; matrix products, arithmetic and copies ran while one was open for 0% of the time, Pallas kernels for 1%

profile of v3, /device:TPU:24, one launch (start us, length us, event | category | flops | bytes accessed | tf_op | source)
XLA Modules:
  0.0 79.2 jit_solution(3716377760045172382)
XLA Ops:
  0.6 1.9 %shard_map.95 = f32[16,72,128]{2,1,0:T(8,128)} custom-call(s32[1,16]{1,0:T(1,128)} %route.1, f32[1,16,8,512]{3,2,1,0:T(8,128)} %flux.3, f32[1,16,512]{2,1,0:T(8,128)} %frac.3, s32[1,16,512]{2,1,0:T(8,128)} %mask.3, f32[1,16,512]{2,1,0:T(8,128)} %area.3), custom_call_target="tpu_custom_call" | custom-call | tf_op jit(solution)/shard_map/pallas_call | solution.py:154
  2.5 0.0 copy-start
  2.5 0.0 copy-start.1
  2.5 0.0 copy-start.2
  2.5 0.0 copy-start.3
  2.5 0.0 copy-start.4
  2.6 0.0 copy-start.5
  2.6 0.0 copy-start.6
  2.6 15.3 %all-to-all-start = ((f32[16,72,128]{2,1,0:T(8,128)}), f32[16,72,128]{2,1,0:T(8,128)S(1)}, u32[]{:S(2)}, u32[]{:S(2)}) async-start(f32[16,72,128]{2,1,0:T(8,128)} %shard_map.95), calls=%async_computation | async-start | bytes 1179648 | tf_op jit(solution)/shard_map/all_to_all | solution.py:174
  17.9 0.0 copy-done
  17.9 0.0 copy-done.1
  17.9 0.0 copy-done.2
  17.9 0.0 copy-done.3
  18.0 0.0 copy-done.4
  18.0 0.0 copy-done.5
  18.0 0.0 copy-done.6
  18.0 0.7 shard_map.96
  18.7 30.0 %all-to-all-done.received = f32[16,72,128]{2,1,0:T(8,128)S(1)} async-done(((f32[16,72,128]{2,1,0:T(8,128)}), f32[16,72,128]{2,1,0:T(8,128)S(1)}, u32[]{:S(2)}, u32[]{:S(2)}) %all-to-all-start) | async-done | bytes 589856 | tf_op jit(solution)/shard_map/all_to_all | solution.py:174
  48.7 0.3 shard_map.97
  49.0 29.2 %psum.7.sums = s32[1,128]{1,0:T(1,128)S(1)} all-reduce(s32[1,128]{1,0:T(1,128)S(1)} %get-tuple-element.7), channel_id=1, replica_groups=mesh['member'=4,'lat_0'=4,'lat_1'=2,'lon'=16] {'lat_0','lat_1','lon'}, use_global_device_ids=true, to_apply=%region_0.0 | all-reduce | flops 128 | bytes 1024 | tf_op jit(solution)/shard_map/psum | solution.py:196
  78.2 1.0 %shard_map.98 = (f32[8,64,128]{2,1,0:T(8,128)}, f32[8]{0:T(128)}) custom-call(s32[1,128]{1,0:T(1,128)S(1)} %psum.7.sums, f32[1,128]{1,0:T(1,128)S(1)} %get-tuple-element.8.scaling, f32[8,64,128]{2,1,0:T(8,128)S(1)} %get-tuple-element.9.quotient, s32[64,128]{1,0:T(8,128)S(1)} %copy-done.1), custom_call_target="tpu_custom_call" | custom-call | tf_op jit(solution)/shard_map/pallas_call | solution.py:197
Async XLA Ops:
  2.5 15.4 %copy-start = (f32[1,16,8,512]{3,2,1,0:T(8,128)S(1)}, f32[1,16,8,512]{3,2,1,0:T(8,128)}, u32[]{:S(2)}) copy-start(f32[1,16,8,512]{3,2,1,0:T(8,128)} %flux.3) | copy-start | bytes 786436
  2.5 15.4 %copy-start.1 = (s32[64,128]{1,0:T(8,128)S(1)}, s32[64,128]{1,0:T(8,128)}, u32[]{:S(2)}) copy-start(s32[64,128]{1,0:T(8,128)} %ocean_wet.5) | copy-start | bytes 98308
  2.5 15.4 %copy-start.2 = (f32[1,16,512]{2,1,0:T(8,128)S(1)}, f32[1,16,512]{2,1,0:T(8,128)}, u32[]{:S(2)}) copy-start(f32[1,16,512]{2,1,0:T(8,128)} %frac.3) | copy-start | bytes 98308
  2.5 15.4 %copy-start.3 = (s32[1,16,512]{2,1,0:T(8,128)S(1)}, s32[1,16,512]{2,1,0:T(8,128)}, u32[]{:S(2)}) copy-start(s32[1,16,512]{2,1,0:T(8,128)} %mask.3) | copy-start | bytes 98308
  2.5 15.4 %copy-start.4 = (f32[1,16,512]{2,1,0:T(8,128)S(1)}, f32[1,16,512]{2,1,0:T(8,128)}, u32[]{:S(2)}) copy-start(f32[1,16,512]{2,1,0:T(8,128)} %area.3) | copy-start | bytes 98308
  2.6 15.4 %copy-start.5 = (f32[64,128]{1,0:T(8,128)S(1)}, f32[64,128]{1,0:T(8,128)}, u32[]{:S(2)}) copy-start(f32[64,128]{1,0:T(8,128)} %ocean_area.3) | copy-start | bytes 98308
  2.6 15.4 %copy-start.6 = (s32[8]{0:T(128)S(1)}, s32[8]{0:T(128)}, u32[]{:S(2)}) copy-start(s32[8]{0:T(128)} %exponent.1) | copy-start | bytes 100
  2.6 46.1 %all-to-all-start = ((f32[16,72,128]{2,1,0:T(8,128)}), f32[16,72,128]{2,1,0:T(8,128)S(1)}, u32[]{:S(2)}, u32[]{:S(2)}) async-start(f32[16,72,128]{2,1,0:T(8,128)} %shard_map.95), calls=%async_computation | async-start | bytes 1179648 | tf_op jit(solution)/shard_map/all_to_all | solution.py:174

commit v4 on v3

--- a/solution.py
+++ b/solution.py
@@ -61,8 +61,9 @@
         tile = target // blocks
         order = taken[tile]
         taken[tile] = order + 1
-        place[b] = 2 * tile + order
-        rows[tile, pl.ds(order, 1), :] = jnp.full((1, LANES), target % blocks, jnp.int32).astype(jnp.float32)
+        at = (tile + (tiles - tiles // 2)) % tiles
+        place[b] = 2 * at + order
+        rows[at, pl.ds(order, 1), :] = jnp.full((1, LANES), target % blocks, jnp.int32).astype(jnp.float32)
     rows_out = pltpu.make_async_copy(rows, chunks.at[:, pl.ds(2 * block_rows, 8)], out_sems.at[blocks])
     rows_out.start()
     frac_in.wait()
@@ -119,12 +120,17 @@
         field = mapped[f * stride : f * stride + height, :]
         per_field.append(jnp.sum(units(cover * field), axis=0, keepdims=True))
         quotient[f] = field / ocean_area[...]
-    sums[...] = sent_sums[...] + spread(jnp.concatenate(per_field, axis=0), TARGET)
+    own = sent_sums[...] + spread(jnp.concatenate(per_field, axis=0), TARGET)
+    for tile in range(sums.shape[0]):
+        sums[tile] = own
 
 
 def correct_kernel(sums, scaling, quotient, ocean_wet, flux, source_total):
     fields = quotient.shape[0]
-    upper = jnp.broadcast_to(sums[...], (8, LANES))
+    whole = sums[0]
+    for tile in range(1, sums.shape[0]):
+        whole = whole + sums[tile]
+    upper = jnp.broadcast_to(whole, (8, LANES))
     lower = pltpu.roll(upper, LANES - LOWER, 1)
     upper = (upper + (lower >> LIMB_BITS)).astype(jnp.float32)
     integral = (upper * float(LIMB_MASK + 1) + (lower & LIMB_MASK).astype(jnp.float32)) * (1.0 / QUANTUM)
@@ -140,6 +146,12 @@
     for f in range(fields):
         flux[f] = cover * scale[f : f + 1] * (quotient[f] + per_field[f : f + 1])
     source_total[...] = (source * scales)[0, :fields]
+
+
+def exchange(chunks):
+    tiles = lax.axis_size("lon")
+    order = [(tiles // 2 + i) % tiles for i in range(tiles)]
+    return lax.all_to_all(chunks, "lon", 0, 0, axis_index_groups=[order], tiled=True)
 
 
 def body(ice_flux, ice_frac, ice_mask, ice_area, route, ocean_area, ocean_wet, exponent):
@@ -171,7 +183,7 @@
         ],
         compiler_params=pltpu.CompilerParams(vmem_limit_bytes=SEND_VMEM_LIMIT),
     )(route, ice_flux, ice_frac, ice_mask, ice_area)
-    received = lax.all_to_all(chunks, "lon", 0, 0, tiled=True)
+    received = exchange(chunks)
     sums, scaling = pl.pallas_call(
         beside_kernel,
         out_shape=(
@@ -186,14 +198,14 @@
         place_kernel,
         out_shape=(
             jax.ShapeDtypeStruct((fields, height, width), jnp.float32),
-            jax.ShapeDtypeStruct((1, LANES), jnp.int32),
+            jax.ShapeDtypeStruct((tiles, 1, LANES), jnp.int32),
         ),
         in_specs=[vmem] * 4,
         out_specs=(vmem, vmem),
         scratch_shapes=[pltpu.VMEM((fields * (height + 8), width), jnp.float32)],
         compiler_params=params,
     )(received, sums, ocean_area, ocean_wet)
-    sums = lax.psum(sums, LAT + ("lon",))
+    sums = exchange(lax.psum(sums, LAT))
     return pl.pallas_call(
         correct_kernel,
         out_shape=(

time: 79.9 us -> 72.9 us (0.912)
  blocking collectives: 29.2 us -> 23.6 us
  waiting for transfers between devices: 30 us -> 25.4 us
  starting transfers between devices: 15.3 us -> 19 us
    psum x1, blocking collectives: 29.2 us -> 9.36 us  [body(): sums = exchange(lax.psum(sums, LAT))]
    all_to_all x0 -> x1, blocking collectives: none -> 14.2 us  [exchange(): lax.all_to_all(chunks, 'lon', 0, 0, axis_index_groups=[order], tiled=True)]
    all_to_all x1, waiting for transfers between devices: 30 us -> 25.4 us  [exchange(): lax.all_to_all(chunks, 'lon', 0, 0, axis_index_groups=[order], tiled=True)]
    all_to_all x1, starting transfers between devices: 15.3 us -> 19 us  [exchange(): lax.all_to_all(chunks, 'lon', 0, 0, axis_index_groups=[order], tiled=True)]
where the time goes in v4:
time: 72.9 us; the launch traced here: 72.6 us
  waiting for transfers between devices  25.4 us (35%)
  blocking collectives  23.6 us (32%)
  starting transfers between devices  19 us (26%)
  Pallas kernels  3.81 us (5%)
  between operations  0.75 us (1%)
    all_to_all x1, waiting for transfers between devices, exchange(): lax.all_to_all(chunks, 'lon', 0, 0, axis_index_groups=[order], tiled=True)  25.4 us
    all_to_all x1, starting transfers between devices, exchange(): lax.all_to_all(chunks, 'lon', 0, 0, axis_index_groups=[order], tiled=True)  19 us
    all_to_all x1, blocking collectives, exchange(): lax.all_to_all(chunks, 'lon', 0, 0, axis_index_groups=[order], tiled=True)  14.2 us
    psum x1, blocking collectives, body(): sums = exchange(lax.psum(sums, LAT))  9.36 us
    pallas_call x1, Pallas kernels, body(): pl.pallas_call(send_kernel, out_shape=jax.ShapeDtypeStruct((tiles, chunk_...  1.85 us
  transfers between devices with their start and end apart: 1, of which 1 were waited for; matrix products, arithmetic and copies ran while one was open for 0% of the time, Pallas kernels for 1%

profile of v4, /device:TPU:24, one launch (start us, length us, event | category | flops | bytes accessed | tf_op | source)
XLA Modules:
  0.0 72.6 jit_solution(15914736752655183920)
XLA Ops:
  0.6 1.9 %shard_map.95 = f32[16,72,128]{2,1,0:T(8,128)} custom-call(s32[1,16]{1,0:T(1,128)} %route.1, f32[1,16,8,512]{3,2,1,0:T(8,128)} %flux.3, f32[1,16,512]{2,1,0:T(8,128)} %frac.3, s32[1,16,512]{2,1,0:T(8,128)} %mask.3, f32[1,16,512]{2,1,0:T(8,128)} %area.3), custom_call_target="tpu_custom_call" | custom-call | tf_op jit(solution)/shard_map/pallas_call | solution.py:166
  2.5 0.0 copy-start
  2.5 0.0 copy-start.1
  2.5 0.0 copy-start.2
  2.5 0.0 copy-start.3
  2.5 0.0 copy-start.4
  2.5 0.0 copy-start.5
  2.6 0.0 copy-start.6
  2.6 19.0 %all-to-all-start = ((f32[16,72,128]{2,1,0:T(8,128)}), f32[16,72,128]{2,1,0:T(8,128)S(1)}, u32[]{:S(2)}, u32[]{:S(2)}) async-start(f32[16,72,128]{2,1,0:T(8,128)} %shard_map.95), calls=%async_computation | async-start | bytes 1179648 | tf_op jit(solution)/shard_map/all_to_all | solution.py:154
  21.6 0.0 copy-done
  21.6 0.0 copy-done.1
  21.6 0.0 copy-done.2
  21.6 0.0 copy-done.3
  21.6 0.0 copy-done.4
  21.6 0.0 copy-done.5
  21.6 0.0 copy-done.6
  21.6 0.7 shard_map.96
  22.3 25.4 %all-to-all-done.received = f32[16,72,128]{2,1,0:T(8,128)S(1)} async-done(((f32[16,72,128]{2,1,0:T(8,128)}), f32[16,72,128]{2,1,0:T(8,128)S(1)}, u32[]{:S(2)}, u32[]{:S(2)}) %all-to-all-start) | async-done | bytes 589856 | tf_op jit(solution)/shard_map/all_to_all | solution.py:154
  47.7 0.3 shard_map.97
  48.0 9.4 %psum.7 = s32[16,1,128]{2,1,0:T(1,128)S(1)} all-reduce(s32[16,1,128]{2,1,0:T(1,128)S(1)} %get-tuple-element.7), channel_id=1, replica_groups=mesh['member'=4,'lat_0'=4,'lat_1'=2,'lon'=16] {'lat_0','lat_1'}, use_global_device_ids=true, to_apply=%region_0.0 | all-reduce | flops 2048 | bytes 16384 | tf_op jit(solution)/shard_map/psum | solution.py:208
  57.4 14.2 %all_to_all.10.sums = s32[16,1,128]{2,1,0:T(1,128)S(1)} all-to-all(s32[16,1,128]{2,1,0:T(1,128)S(1)} %psum.7), channel_id=1, replica_groups={{8,9,10,11,12,13,14,15,0,1,2,3,4,5,6,7},{24,25,26,27,28,29,30,31,16,17,..., dimensions={0} | all-to-all | bytes 16384 | tf_op jit(solution)/shard_map/all_to_all | solution.py:154
  71.6 1.0 %shard_map.98 = (f32[8,64,128]{2,1,0:T(8,128)}, f32[8]{0:T(128)}) custom-call(s32[16,1,128]{2,1,0:T(1,128)S(1)} %all_to_all.10.sums, f32[1,128]{1,0:T(1,128)S(1)} %get-tuple-element.8.scaling, f32[8,64,128]{2,1,0:T(8,128)S(1)} %get-tuple-element.9.quotient, s32[64,128]{1,0:T(8,128)S(1)} %copy-done.1), custom_call_target="tpu_custom_call" | custom-call | tf_op jit(solution)/shard_map/pallas_call | solution.py:209
Async XLA Ops:
  2.5 19.1 %copy-start = (f32[1,16,8,512]{3,2,1,0:T(8,128)S(1)}, f32[1,16,8,512]{3,2,1,0:T(8,128)}, u32[]{:S(2)}) copy-start(f32[1,16,8,512]{3,2,1,0:T(8,128)} %flux.3) | copy-start | bytes 786436
  2.5 19.1 %copy-start.1 = (s32[64,128]{1,0:T(8,128)S(1)}, s32[64,128]{1,0:T(8,128)}, u32[]{:S(2)}) copy-start(s32[64,128]{1,0:T(8,128)} %ocean_wet.5) | copy-start | bytes 98308
  2.5 19.1 %copy-start.2 = (f32[1,16,512]{2,1,0:T(8,128)S(1)}, f32[1,16,512]{2,1,0:T(8,128)}, u32[]{:S(2)}) copy-start(f32[1,16,512]{2,1,0:T(8,128)} %frac.3) | copy-start | bytes 98308
  2.5 19.1 %copy-start.3 = (s32[1,16,512]{2,1,0:T(8,128)S(1)}, s32[1,16,512]{2,1,0:T(8,128)}, u32[]{:S(2)}) copy-start(s32[1,16,512]{2,1,0:T(8,128)} %mask.3) | copy-start | bytes 98308
  2.5 19.1 %copy-start.4 = (f32[1,16,512]{2,1,0:T(8,128)S(1)}, f32[1,16,512]{2,1,0:T(8,128)}, u32[]{:S(2)}) copy-start(f32[1,16,512]{2,1,0:T(8,128)} %area.3) | copy-start | bytes 98308
  2.5 19.1 %copy-start.5 = (f32[64,128]{1,0:T(8,128)S(1)}, f32[64,128]{1,0:T(8,128)}, u32[]{:S(2)}) copy-start(f32[64,128]{1,0:T(8,128)} %ocean_area.3) | copy-start | bytes 98308
  2.6 19.1 %copy-start.6 = (s32[8]{0:T(128)S(1)}, s32[8]{0:T(128)}, u32[]{:S(2)}) copy-start(s32[8]{0:T(128)} %exponent.1) | copy-start | bytes 100
  2.6 45.2 %all-to-all-start = ((f32[16,72,128]{2,1,0:T(8,128)}), f32[16,72,128]{2,1,0:T(8,128)S(1)}, u32[]{:S(2)}, u32[]{:S(2)}) async-start(f32[16,72,128]{2,1,0:T(8,128)} %shard_map.95), calls=%async_computation | async-start | bytes 1179648 | tf_op jit(solution)/shard_map/all_to_all | solution.py:154

commit v5 on v4

--- a/solution.py
+++ b/solution.py
@@ -34,11 +34,12 @@
     return jnp.sum(placed, axis=0, keepdims=True).astype(jnp.int32)
 
 
-def send_kernel(route, flux, frac, mask, area, chunks, route_s, flux_v, frac_v, mask_v, area_v, staged, rows, taken, place, in_sems, out_sems):
+def send_kernel(route, flux, frac, mask, area, chunks, route_s, flux_v, frac_v, mask_v, area_v, taken, in_sems):
     blocks, fields, cells = flux_v.shape
-    tiles = chunks.shape[0]
+    tiles = taken.shape[0]
     band = cells // LANES
     block_rows = band * fields
+    chunk_rows = chunks.shape[0] // tiles
     route_in = pltpu.make_async_copy(route.at[0], route_s, in_sems.at[0])
     frac_in = pltpu.make_async_copy(frac.at[0], frac_v, in_sems.at[1])
     mask_in = pltpu.make_async_copy(mask.at[0], mask_v, in_sems.at[2])
@@ -50,40 +51,31 @@
         flux_in.append(pltpu.make_async_copy(flux.at[0, part], flux_v.at[part], in_sems.at[4 + p]))
     for copy in [route_in, frac_in, mask_in, area_in] + flux_in:
         copy.start()
+    lane = lax.broadcasted_iota(jnp.int32, (1, LANES), 1)
+    nobody = jnp.full((1, LANES), float(blocks), jnp.float32)
     for tile in range(tiles):
         taken[tile] = 0
-    nobody = jnp.full((8, LANES), float(blocks), jnp.float32)
-    for tile in range(tiles):
-        rows[tile] = nobody
+        chunks[tile * chunk_rows + chunk_rows - 1 : (tile + 1) * chunk_rows, :] = nobody
     route_in.wait()
+    frac_in.wait()
+    mask_in.wait()
+    area_in.wait()
+    amount = area_v[...] * frac_v[...] * mask_v[...].astype(jnp.float32)
     for b in range(blocks):
+        if b % piece == 0:
+            flux_in[b // piece].wait()
         target = route_s[b]
         tile = target // blocks
         order = taken[tile]
         taken[tile] = order + 1
-        at = (tile + (tiles - tiles // 2)) % tiles
-        place[b] = 2 * at + order
-        rows[at, pl.ds(order, 1), :] = jnp.full((1, LANES), target % blocks, jnp.int32).astype(jnp.float32)
-    rows_out = pltpu.make_async_copy(rows, chunks.at[:, pl.ds(2 * block_rows, 8)], out_sems.at[blocks])
-    rows_out.start()
-    frac_in.wait()
-    mask_in.wait()
-    area_in.wait()
-    amount = area_v[...] * frac_v[...] * mask_v[...].astype(jnp.float32)
-    blocks_out = []
-    for b in range(blocks):
-        if b % piece == 0:
-            flux_in[b // piece].wait()
+        chunk = ((tile + (tiles - tiles // 2)) % tiles) * chunk_rows
         carried = flux_v[b] * amount[b : b + 1]
+        first = chunk + order * block_rows
         for r in range(band):
-            staged[b, r * fields : (r + 1) * fields, :] = carried[:, r * LANES : (r + 1) * LANES]
-        first = pl.multiple_of((place[b] % 2) * block_rows, block_rows)
-        to = chunks.at[place[b] // 2, pl.ds(first, block_rows)]
-        blocks_out.append(pltpu.make_async_copy(staged.at[b], to, out_sems.at[b]))
-        blocks_out[b].start()
-    rows_out.wait()
-    for copy in blocks_out:
-        copy.wait()
+            chunks[pl.ds(first + r * fields, fields), :] = carried[:, r * LANES : (r + 1) * LANES]
+        last = pl.ds(chunk + chunk_rows - 1, 1)
+        row = jnp.full((1, LANES), target % blocks, jnp.int32).astype(jnp.float32)
+        chunks[last, :] = jnp.where(lane == order, row, chunks[last, :])
 
 
 def beside_kernel(exponent, flux, frac, mask, area, ocean_area, ocean_wet, sums, scaling):
@@ -106,14 +98,16 @@
 def place_kernel(received, sent_sums, ocean_area, ocean_wet, quotient, sums, mapped):
     fields, height, width = quotient.shape
     stride = mapped.shape[0] // fields
-    band = (received.shape[1] - 8) // (2 * fields)
-    for s in range(received.shape[0]):
+    tiles = sums.shape[0]
+    band = received.shape[0] // tiles // (2 * fields)
+    chunk_rows = received.shape[0] // tiles
+    for tile in range(tiles):
+        chunk = tile * chunk_rows
         for order in range(2):
-            at = (2 * s + order) * band * fields
-            row = received[s, 2 * band * fields + order, 0].astype(jnp.int32)
+            row = received[chunk + chunk_rows - 1, order].astype(jnp.int32)
             for r in range(band):
-                first = (order * band + r) * fields
-                mapped[pl.ds(row * band + r, fields, stride), :] = received[s, first : first + fields, :]
+                first = chunk + (order * band + r) * fields
+                mapped[pl.ds(row * band + r, fields, stride), :] = received[first : first + fields, :]
     cover = ocean_wet[...].astype(jnp.float32)
     per_field = []
     for f in range(fields):
@@ -158,32 +152,28 @@
     blocks, fields, cells = ice_flux.shape[1:]
     height, width = ocean_area.shape
     tiles = lax.axis_size("lon")
-    chunk_rows = 2 * fields * cells // LANES + 8
+    chunk_rows = 2 * fields * cells // LANES + 1
     vmem = pl.BlockSpec(memory_space=pltpu.VMEM)
     smem = pl.BlockSpec(memory_space=pltpu.SMEM)
     hbm = pl.BlockSpec(memory_space=pltpu.HBM)
     params = pltpu.CompilerParams(vmem_limit_bytes=VMEM_LIMIT)
     chunks = pl.pallas_call(
         send_kernel,
-        out_shape=jax.ShapeDtypeStruct((tiles, chunk_rows, LANES), jnp.float32),
+        out_shape=jax.ShapeDtypeStruct((tiles * chunk_rows, LANES), jnp.float32),
         in_specs=[hbm] * 5,
-        out_specs=hbm,
+        out_specs=vmem,
         scratch_shapes=[
             pltpu.SMEM((blocks,), jnp.int32),
             pltpu.VMEM((blocks, fields, cells), jnp.float32),
             pltpu.VMEM((blocks, cells), jnp.float32),
             pltpu.VMEM((blocks, cells), jnp.int32),
             pltpu.VMEM((blocks, cells), jnp.float32),
-            pltpu.VMEM((blocks, fields * cells // LANES, LANES), jnp.float32),
-            pltpu.VMEM((tiles, 8, LANES), jnp.float32),
             pltpu.SMEM((tiles,), jnp.int32),
-            pltpu.SMEM((blocks,), jnp.int32),
             pltpu.SemaphoreType.DMA((4 + PIECES,)),
-            pltpu.SemaphoreType.DMA((blocks + 1,)),
         ],
         compiler_params=pltpu.CompilerParams(vmem_limit_bytes=SEND_VMEM_LIMIT),
     )(route, ice_flux, ice_frac, ice_mask, ice_area)
-    received = exchange(chunks)
+    received = exchange(chunks.reshape(tiles, chunk_rows, 1, LANES)).reshape(tiles * chunk_rows, LANES)
     sums, scaling = pl.pallas_call(
         beside_kernel,
         out_shape=(

time: 72.9 us -> 70.6 us (0.968)
  waiting for transfers between devices: 25.4 us -> 22.9 us
    all_to_all x1, waiting for transfers between devices: 25.4 us -> 22.9 us  [exchange(): lax.all_to_all(chunks, 'lon', 0, 0, axis_index_groups=[order], tiled=True)]
where the time goes in v5:
time: 70.6 us; the launch traced here: 70.3 us
  blocking collectives  23.6 us (33%)
  waiting for transfers between devices  22.9 us (32%)
  starting transfers between devices  19 us (27%)
  Pallas kernels  3.98 us (6%)
  between operations  0.75 us (1%)
    all_to_all x1, waiting for transfers between devices, exchange(): lax.all_to_all(chunks, 'lon', 0, 0, axis_index_groups=[order], tiled=True)  22.9 us
    all_to_all x1, starting transfers between devices, exchange(): lax.all_to_all(chunks, 'lon', 0, 0, axis_index_groups=[order], tiled=True)  19 us
    all_to_all x1, blocking collectives, exchange(): lax.all_to_all(chunks, 'lon', 0, 0, axis_index_groups=[order], tiled=True)  14.2 us
    psum x1, blocking collectives, body(): sums = exchange(lax.psum(sums, LAT))  9.37 us
    pallas_call x1, Pallas kernels, body(): pl.pallas_call(send_kernel, out_shape=jax.ShapeDtypeStruct((tiles * chunk...  1.95 us
  transfers between devices with their start and end apart: 1, of which 1 were waited for; matrix products, arithmetic and copies ran while one was open for 0% of the time, Pallas kernels for 1%

profile of v5, /device:TPU:24, one launch (start us, length us, event | category | flops | bytes accessed | tf_op | source)
XLA Modules:
  0.0 70.3 jit_solution(1391296131161251809)
XLA Ops:
  0.6 2.0 %shard_map.95 = f32[1040,128]{1,0:T(8,128)} custom-call(s32[1,16]{1,0:T(1,128)} %route.1, f32[1,16,8,512]{3,2,1,0:T(8,128)} %flux.3, f32[1,16,512]{2,1,0:T(8,128)} %frac.3, s32[1,16,512]{2,1,0:T(8,128)} %mask.3, f32[1,16,512]{2,1,0:T(8,128)} %area.3), custom_call_target="tpu_custom_call" | custom-call | tf_op jit(solution)/shard_map/pallas_call | solution.py:160
  2.6 0.0 copy-start
  2.6 0.0 copy-start.1
  2.6 0.0 copy-start.2
  2.6 0.0 copy-start.3
  2.6 0.0 copy-start.4
  2.7 0.0 copy-start.5
  2.7 0.0 copy-start.6
  2.7 19.0 %all-to-all-start = ((f32[16,65,1,128]{3,2,1,0:T(1,128)}), f32[16,65,1,128]{3,2,1,0:T(1,128)S(1)}, u32[]{:S(2)}, u32[]{:S(2)}) async-start(f32[16,65,1,128]{3,2,1,0:T(1,128)} %bitcast.3), calls=%async_computation | async-start | bytes 1064960 | tf_op jit(solution)/shard_map/all_to_all | solution.py:148
  21.7 0.0 copy-done
  21.7 0.0 copy-done.1
  21.7 0.0 copy-done.2
  21.7 0.0 copy-done.3
  21.7 0.0 copy-done.4
  21.7 0.0 copy-done.5
  21.7 0.0 copy-done.6
  21.7 0.7 shard_map.96
  22.4 22.9 %all-to-all-done = f32[16,65,1,128]{3,2,1,0:T(1,128)S(1)} async-done(((f32[16,65,1,128]{3,2,1,0:T(1,128)}), f32[16,65,1,128]{3,2,1,0:T(1,128)S(1)}, u32[]{:S(2)}, u32[]{:S(2)}) %all-to-all-start) | async-done | bytes 532512 | tf_op jit(solution)/shard_map/all_to_all | solution.py:148
  45.4 0.3 shard_map.97
  45.7 9.4 %psum.7 = s32[16,1,128]{2,1,0:T(1,128)S(1)} all-reduce(s32[16,1,128]{2,1,0:T(1,128)S(1)} %get-tuple-element.7), channel_id=1, replica_groups=mesh['member'=4,'lat_0'=4,'lat_1'=2,'lon'=16] {'lat_0','lat_1'}, use_global_device_ids=true, to_apply=%region_0.0 | all-reduce | flops 2048 | bytes 16384 | tf_op jit(solution)/shard_map/psum | solution.py:198
  55.1 14.2 %all_to_all.10.sums = s32[16,1,128]{2,1,0:T(1,128)S(1)} all-to-all(s32[16,1,128]{2,1,0:T(1,128)S(1)} %psum.7), channel_id=1, replica_groups={{8,9,10,11,12,13,14,15,0,1,2,3,4,5,6,7},{24,25,26,27,28,29,30,31,16,17,..., dimensions={0} | all-to-all | bytes 16384 | tf_op jit(solution)/shard_map/all_to_all | solution.py:148
  69.3 1.0 %shard_map.98 = (f32[8,64,128]{2,1,0:T(8,128)}, f32[8]{0:T(128)}) custom-call(s32[16,1,128]{2,1,0:T(1,128)S(1)} %all_to_all.10.sums, f32[1,128]{1,0:T(1,128)S(1)} %get-tuple-element.8.scaling, f32[8,64,128]{2,1,0:T(8,128)S(1)} %get-tuple-element.9.quotient, s32[64,128]{1,0:T(8,128)S(1)} %copy-done.1), custom_call_target="tpu_custom_call" | custom-call | tf_op jit(solution)/shard_map/pallas_call | solution.py:199
Async XLA Ops:
  2.6 19.1 %copy-start = (f32[1,16,8,512]{3,2,1,0:T(8,128)S(1)}, f32[1,16,8,512]{3,2,1,0:T(8,128)}, u32[]{:S(2)}) copy-start(f32[1,16,8,512]{3,2,1,0:T(8,128)} %flux.3) | copy-start | bytes 786436
  2.6 19.1 %copy-start.1 = (s32[64,128]{1,0:T(8,128)S(1)}, s32[64,128]{1,0:T(8,128)}, u32[]{:S(2)}) copy-start(s32[64,128]{1,0:T(8,128)} %ocean_wet.5) | copy-start | bytes 98308
  2.6 19.1 %copy-start.2 = (f32[1,16,512]{2,1,0:T(8,128)S(1)}, f32[1,16,512]{2,1,0:T(8,128)}, u32[]{:S(2)}) copy-start(f32[1,16,512]{2,1,0:T(8,128)} %frac.3) | copy-start | bytes 98308
  2.6 19.1 %copy-start.3 = (s32[1,16,512]{2,1,0:T(8,128)S(1)}, s32[1,16,512]{2,1,0:T(8,128)}, u32[]{:S(2)}) copy-start(s32[1,16,512]{2,1,0:T(8,128)} %mask.3) | copy-start | bytes 98308
  2.6 19.1 %copy-start.4 = (f32[1,16,512]{2,1,0:T(8,128)S(1)}, f32[1,16,512]{2,1,0:T(8,128)}, u32[]{:S(2)}) copy-start(f32[1,16,512]{2,1,0:T(8,128)} %area.3) | copy-start | bytes 98308
  2.7 19.1 %copy-start.5 = (f32[64,128]{1,0:T(8,128)S(1)}, f32[64,128]{1,0:T(8,128)}, u32[]{:S(2)}) copy-start(f32[64,128]{1,0:T(8,128)} %ocean_area.3) | copy-start | bytes 98308
  2.7 19.1 %copy-start.6 = (s32[8]{0:T(128)S(1)}, s32[8]{0:T(128)}, u32[]{:S(2)}) copy-start(s32[8]{0:T(128)} %exponent.1) | copy-start | bytes 100
  2.7 42.7 %all-to-all-start = ((f32[16,65,1,128]{3,2,1,0:T(1,128)}), f32[16,65,1,128]{3,2,1,0:T(1,128)S(1)}, u32[]{:S(2)}, u32[]{:S(2)}) async-start(f32[16,65,1,128]{3,2,1,0:T(1,128)} %bitcast.3), calls=%async_computation | async-start | bytes 1064960 | tf_op jit(solution)/shard_map/all_to_all | solution.py:148

commit v6 on v5

--- a/solution.py
+++ b/solution.py
@@ -1,3 +1,5 @@
+import functools
+
 import jax
 import jax.numpy as jnp
 from jax import lax
@@ -7,7 +9,6 @@
 from jax.sharding import PartitionSpec as P
 
 MEMBER_LAT = ("member", "lat_0", "lat_1")
-LAT = ("lat_0", "lat_1")
 
 QUANTUM = 1024.0
 LIMB_BITS = 16
@@ -55,7 +56,7 @@
     nobody = jnp.full((1, LANES), float(blocks), jnp.float32)
     for tile in range(tiles):
         taken[tile] = 0
-        chunks[tile * chunk_rows + chunk_rows - 1 : (tile + 1) * chunk_rows, :] = nobody
+        chunks[tile * chunk_rows : tile * chunk_rows + 1, :] = nobody
     route_in.wait()
     frac_in.wait()
     mask_in.wait()
@@ -70,12 +71,12 @@
         taken[tile] = order + 1
         chunk = ((tile + (tiles - tiles // 2)) % tiles) * chunk_rows
         carried = flux_v[b] * amount[b : b + 1]
-        first = chunk + order * block_rows
+        first = chunk + 1 + order * block_rows
         for r in range(band):
             chunks[pl.ds(first + r * fields, fields), :] = carried[:, r * LANES : (r + 1) * LANES]
-        last = pl.ds(chunk + chunk_rows - 1, 1)
+        head = pl.ds(chunk, 1)
         row = jnp.full((1, LANES), target % blocks, jnp.int32).astype(jnp.float32)
-        chunks[last, :] = jnp.where(lane == order, row, chunks[last, :])
+        chunks[head, :] = jnp.where(lane == order, row, chunks[head, :])
 
 
 def beside_kernel(exponent, flux, frac, mask, area, ocean_area, ocean_wet, sums, scaling):
@@ -95,18 +96,17 @@
     scaling[...] = scales.astype(jnp.float32)
 
 
-def place_kernel(received, sent_sums, ocean_area, ocean_wet, quotient, sums, mapped):
+def place_kernel(tiles, received, sent_sums, ocean_area, ocean_wet, quotient, sums, mapped):
     fields, height, width = quotient.shape
-    stride = mapped.shape[0] // fields
-    tiles = sums.shape[0]
+    stride = mapped.shape[0] // (fields + 1)
     band = received.shape[0] // tiles // (2 * fields)
     chunk_rows = received.shape[0] // tiles
     for tile in range(tiles):
         chunk = tile * chunk_rows
         for order in range(2):
-            row = received[chunk + chunk_rows - 1, order].astype(jnp.int32)
+            row = received[chunk, order].astype(jnp.int32)
             for r in range(band):
-                first = chunk + (order * band + r) * fields
+                first = chunk + 1 + (order * band + r) * fields
                 mapped[pl.ds(row * band + r, fields, stride), :] = received[first : first + fields, :]
     cover = ocean_wet[...].astype(jnp.float32)
     per_field = []
@@ -114,9 +114,7 @@
         field = mapped[f * stride : f * stride + height, :]
         per_field.append(jnp.sum(units(cover * field), axis=0, keepdims=True))
         quotient[f] = field / ocean_area[...]
-    own = sent_sums[...] + spread(jnp.concatenate(per_field, axis=0), TARGET)
-    for tile in range(sums.shape[0]):
-        sums[tile] = own
+    sums[...] = sent_sums[...] + spread(jnp.concatenate(per_field, axis=0), TARGET)
 
 
 def correct_kernel(sums, scaling, quotient, ocean_wet, flux, source_total):
@@ -142,10 +140,12 @@
     source_total[...] = (source * scales)[0, :fields]
 
 
-def exchange(chunks):
+def exchange(chunks, rows=()):
     tiles = lax.axis_size("lon")
-    order = [(tiles // 2 + i) % tiles for i in range(tiles)]
-    return lax.all_to_all(chunks, "lon", 0, 0, axis_index_groups=[order], tiled=True)
+    order = [
+        row * tiles + (tiles // 2 + i) % tiles for i in range(tiles) for row in range(chunks.shape[0] // tiles)
+    ]
+    return lax.all_to_all(chunks, rows + ("lon",), 0, 0, axis_index_groups=[order], tiled=True)
 
 
 def body(ice_flux, ice_frac, ice_mask, ice_area, route, ocean_area, ocean_wet, exponent):
@@ -185,17 +185,19 @@
         compiler_params=params,
     )(exponent, ice_flux, ice_frac, ice_mask, ice_area, ocean_area, ocean_wet)
     quotient, sums = pl.pallas_call(
-        place_kernel,
+        functools.partial(place_kernel, tiles),
         out_shape=(
             jax.ShapeDtypeStruct((fields, height, width), jnp.float32),
-            jax.ShapeDtypeStruct((tiles, 1, LANES), jnp.int32),
+            jax.ShapeDtypeStruct((1, LANES), jnp.int32),
         ),
         in_specs=[vmem] * 4,
         out_specs=(vmem, vmem),
-        scratch_shapes=[pltpu.VMEM((fields * (height + 8), width), jnp.float32)],
+        scratch_shapes=[pltpu.VMEM(((fields + 1) * (height + 8), width), jnp.float32)],
         compiler_params=params,
     )(received, sums, ocean_area, ocean_wet)
-    sums = exchange(lax.psum(sums, LAT))
+    sums = lax.psum(sums, "lat_1")
+    copies = lax.axis_size("lat_0") * tiles
+    sums = exchange(jnp.broadcast_to(sums[None], (copies, 1, LANES)), ("lat_0",))
     return pl.pallas_call(
         correct_kernel,
         out_shape=(

time: 70.6 us -> 68.8 us (0.975)
  blocking collectives: 23.6 us -> 21.7 us
    psum x1, blocking collectives: 9.37 us -> 1.81 us  [body(): sums = lax.psum(sums, 'lat_1')]
    all_to_all x1, blocking collectives: 14.2 us -> 19.9 us  [exchange(): lax.all_to_all(chunks, rows + ('lon',), 0, 0, axis_index_groups=[order],...]
where the time goes in v6:
time: 68.8 us; the launch traced here: 68.5 us
  waiting for transfers between devices  22.9 us (33%)
  blocking collectives  21.7 us (32%)
  starting transfers between devices  19 us (28%)
  Pallas kernels  4.03 us (6%)
  between operations  0.75 us (1%)
    all_to_all x1, waiting for transfers between devices, exchange(): lax.all_to_all(chunks, rows + ('lon',), 0, 0, axis_index_groups=[order],...  22.9 us
    all_to_all x1, blocking collectives, exchange(): lax.all_to_all(chunks, rows + ('lon',), 0, 0, axis_index_groups=[order],...  19.9 us
    all_to_all x1, starting transfers between devices, exchange(): lax.all_to_all(chunks, rows + ('lon',), 0, 0, axis_index_groups=[order],...  19 us
    pallas_call x1, Pallas kernels, body(): pl.pallas_call(send_kernel, out_shape=jax.ShapeDtypeStruct((tiles * chunk...  1.95 us
    psum x1, blocking collectives, body(): sums = lax.psum(sums, 'lat_1')  1.81 us
  transfers between devices with their start and end apart: 1, of which 1 were waited for; matrix products, arithmetic and copies ran while one was open for 0% of the time, Pallas kernels for 1%

profile of v6, /device:TPU:24, one launch (start us, length us, event | category | flops | bytes accessed | tf_op | source)
XLA Modules:
  0.0 68.5 jit_solution(6316285274486050739)
XLA Ops:
  0.6 2.0 %shard_map.95 = f32[1040,128]{1,0:T(8,128)} custom-call(s32[1,16]{1,0:T(1,128)} %route.1, f32[1,16,8,512]{3,2,1,0:T(8,128)} %flux.3, f32[1,16,512]{2,1,0:T(8,128)} %frac.3, s32[1,16,512]{2,1,0:T(8,128)} %mask.3, f32[1,16,512]{2,1,0:T(8,128)} %area.3), custom_call_target="tpu_custom_call" | custom-call | tf_op jit(solution)/shard_map/pallas_call | solution.py:160
  2.6 0.0 copy-start
  2.6 0.0 copy-start.1
  2.6 0.0 copy-start.2
  2.6 0.0 copy-start.3
  2.6 0.0 copy-start.4
  2.7 0.0 copy-start.5
  2.7 0.0 copy-start.6
  2.7 19.0 %all-to-all-start = ((f32[16,65,1,128]{3,2,1,0:T(1,128)}), f32[16,65,1,128]{3,2,1,0:T(1,128)S(1)}, u32[]{:S(2)}, u32[]{:S(2)}) async-start(f32[16,65,1,128]{3,2,1,0:T(1,128)} %bitcast.5), calls=%async_computation | async-start | bytes 1064960 | tf_op jit(solution)/shard_map/all_to_all | solution.py:148
  21.7 0.0 copy-done
  21.7 0.0 copy-done.1
  21.7 0.0 copy-done.2
  21.7 0.0 copy-done.3
  21.7 0.0 copy-done.4
  21.7 0.0 copy-done.5
  21.7 0.0 copy-done.6
  21.7 0.7 %shard_map.96 = (s32[1,128]{1,0:T(1,128)S(1)}, f32[1,128]{1,0:T(1,128)S(1)}) custom-call(s32[8]{0:T(128)S(1)} %copy-done.6, f32[1,16,8,512]{3,2,1,0:T(8,128)S(1)} %copy-done, f32[1,16,512]{2,1,0:T(8,128)S(1)} %copy-done.2, s32[1,16,512]{2,1,0:T(8,128)S(1)} %copy-done.3, f32[1,16,512]{2,1,0:T(8,128)S(1)} %copy-done.4, f32[64,128]{1,0:T(8,128)S(1)} %copy-done.5, ...), custom_call_target="tpu_custom_call" | custom-call | tf_op jit(solution)/shard_map/pallas_call | solution.py:177
  22.4 22.9 %all-to-all-done = f32[16,65,1,128]{3,2,1,0:T(1,128)S(1)} async-done(((f32[16,65,1,128]{3,2,1,0:T(1,128)}), f32[16,65,1,128]{3,2,1,0:T(1,128)S(1)}, u32[]{:S(2)}, u32[]{:S(2)}) %all-to-all-start) | async-done | bytes 532512 | tf_op jit(solution)/shard_map/all_to_all | solution.py:148
  45.4 0.3 shard_map.97
  45.7 1.8 %psum.7 = s32[128]{0:T(128)S(1)} all-reduce(s32[128]{0:T(128)S(1)} %bitcast.4), channel_id=1, replica_groups=mesh['member'=4,'lat_0'=4,'lat_1'=2,'lon'=16] {'lat_1'}, use_global_device_ids=true, to_apply=%region_0.0 | all-reduce | flops 128 | bytes 1024 | tf_op jit(solution)/shard_map/psum | solution.py:198
  47.6 19.9 %all_to_all.10.sums = s32[64,1,128]{2,1,0:T(1,128)S(1)} all-to-all(s32[64,1,128]{2,1,0:T(1,128)S(1)} %broadcast_in_dim.9), channel_id=1, replica_groups={{8,40,72,104,9,41,73,105,10,42,74,106,11,43,75,107,12,44,76,108,13,45,7..., dimensions={0} | all-to-all | bytes 65536 | tf_op jit(solution)/shard_map/all_to_all | solution.py:148
  67.4 1.0 %shard_map.98 = (f32[8,64,128]{2,1,0:T(8,128)}, f32[8]{0:T(128)}) custom-call(s32[64,1,128]{2,1,0:T(1,128)S(1)} %all_to_all.10.sums, f32[1,128]{1,0:T(1,128)S(1)} %get-tuple-element.8.scaling, f32[8,64,128]{2,1,0:T(8,128)S(1)} %get-tuple-element.9.quotient, s32[64,128]{1,0:T(8,128)S(1)} %copy-done.1), custom_call_target="tpu_custom_call" | custom-call | tf_op jit(solution)/shard_map/pallas_call | solution.py:201
  (1 shorter events, 0.0 us)
Async XLA Ops:
  2.6 19.1 %copy-start = (f32[1,16,8,512]{3,2,1,0:T(8,128)S(1)}, f32[1,16,8,512]{3,2,1,0:T(8,128)}, u32[]{:S(2)}) copy-start(f32[1,16,8,512]{3,2,1,0:T(8,128)} %flux.3) | copy-start | bytes 786436
  2.6 19.1 %copy-start.1 = (s32[64,128]{1,0:T(8,128)S(1)}, s32[64,128]{1,0:T(8,128)}, u32[]{:S(2)}) copy-start(s32[64,128]{1,0:T(8,128)} %ocean_wet.5) | copy-start | bytes 98308
  2.6 19.1 %copy-start.2 = (f32[1,16,512]{2,1,0:T(8,128)S(1)}, f32[1,16,512]{2,1,0:T(8,128)}, u32[]{:S(2)}) copy-start(f32[1,16,512]{2,1,0:T(8,128)} %frac.3) | copy-start | bytes 98308
  2.6 19.1 %copy-start.3 = (s32[1,16,512]{2,1,0:T(8,128)S(1)}, s32[1,16,512]{2,1,0:T(8,128)}, u32[]{:S(2)}) copy-start(s32[1,16,512]{2,1,0:T(8,128)} %mask.3) | copy-start | bytes 98308
  2.6 19.1 %copy-start.4 = (f32[1,16,512]{2,1,0:T(8,128)S(1)}, f32[1,16,512]{2,1,0:T(8,128)}, u32[]{:S(2)}) copy-start(f32[1,16,512]{2,1,0:T(8,128)} %area.3) | copy-start | bytes 98308
  2.7 19.1 %copy-start.5 = (f32[64,128]{1,0:T(8,128)S(1)}, f32[64,128]{1,0:T(8,128)}, u32[]{:S(2)}) copy-start(f32[64,128]{1,0:T(8,128)} %ocean_area.3) | copy-start | bytes 98308
  2.7 19.1 %copy-start.6 = (s32[8]{0:T(128)S(1)}, s32[8]{0:T(128)}, u32[]{:S(2)}) copy-start(s32[8]{0:T(128)} %exponent.1) | copy-start | bytes 100
  2.7 42.7 %all-to-all-start = ((f32[16,65,1,128]{3,2,1,0:T(1,128)}), f32[16,65,1,128]{3,2,1,0:T(1,128)S(1)}, u32[]{:S(2)}, u32[]{:S(2)}) async-start(f32[16,65,1,128]{3,2,1,0:T(1,128)} %bitcast.5), calls=%async_computation | async-start | bytes 1064960 | tf_op jit(solution)/shard_map/all_to_all | solution.py:148

commit v7 on v6

--- a/solution.py
+++ b/solution.py
@@ -69,7 +69,7 @@
         tile = target // blocks
         order = taken[tile]
         taken[tile] = order + 1
-        chunk = ((tile + (tiles - tiles // 2)) % tiles) * chunk_rows
+        chunk = ((tile + (tiles - ring_start(tiles))) % tiles) * chunk_rows
         carried = flux_v[b] * amount[b : b + 1]
         first = chunk + 1 + order * block_rows
         for r in range(band):
@@ -140,12 +140,23 @@
     source_total[...] = (source * scales)[0, :fields]
 
 
-def exchange(chunks, rows=()):
-    tiles = lax.axis_size("lon")
+def ring_start(tiles):
+    return tiles * 5 // 8
+
+
+def exchange(chunks):
+    tiles = chunks.shape[0]
+    order = [(ring_start(tiles) + i) % tiles for i in range(tiles)]
+    return lax.all_to_all(chunks, "lon", 0, 0, axis_index_groups=[order], tiled=True)
+
+
+def gathered(row):
+    columns, tiles = lax.axis_size("lat_0"), lax.axis_size("lon")
     order = [
-        row * tiles + (tiles // 2 + i) % tiles for i in range(tiles) for row in range(chunks.shape[0] // tiles)
+        (columns // 2 + j) % columns * tiles + (tiles // 2 + i) % tiles for i in range(tiles) for j in range(columns)
     ]
-    return lax.all_to_all(chunks, rows + ("lon",), 0, 0, axis_index_groups=[order], tiled=True)
+    copies = jnp.broadcast_to(row[None], (columns * tiles, *row.shape))
+    return lax.all_to_all(copies, ("lat_0", "lon"), 0, 0, axis_index_groups=[order], tiled=True)
 
 
 def body(ice_flux, ice_frac, ice_mask, ice_area, route, ocean_area, ocean_wet, exponent):
@@ -195,9 +206,7 @@
         scratch_shapes=[pltpu.VMEM(((fields + 1) * (height + 8), width), jnp.float32)],
         compiler_params=params,
     )(received, sums, ocean_area, ocean_wet)
-    sums = lax.psum(sums, "lat_1")
-    copies = lax.axis_size("lat_0") * tiles
-    sums = exchange(jnp.broadcast_to(sums[None], (copies, 1, LANES)), ("lat_0",))
+    sums = gathered(lax.psum(sums, "lat_1"))
     return pl.pallas_call(
         correct_kernel,
         out_shape=(

time: 68.8 us -> 66.7 us (0.969)
  starting transfers between devices: 19 us -> 17.2 us
  blocking collectives: 21.7 us -> 20.1 us
  waiting for transfers between devices: 22.9 us -> 24.3 us
    all_to_all x1, starting transfers between devices: 19 us -> 17.2 us  [exchange(): lax.all_to_all(chunks, 'lon', 0, 0, axis_index_groups=[order], tiled=True)]
    all_to_all x1, blocking collectives: 19.9 us -> 18.3 us  [gathered(): lax.all_to_all(copies, ('lat_0', 'lon'), 0, 0, axis_index_groups=[order],...]
    all_to_all x1, waiting for transfers between devices: 22.9 us -> 24.3 us  [exchange(): lax.all_to_all(chunks, 'lon', 0, 0, axis_index_groups=[order], tiled=True)]
where the time goes in v7:
time: 66.7 us; the launch traced here: 66.4 us
  waiting for transfers between devices  24.3 us (36%)
  blocking collectives  20.1 us (30%)
  starting transfers between devices  17.2 us (26%)
  Pallas kernels  4.02 us (6%)
  between operations  0.75 us (1%)
    all_to_all x1, waiting for transfers between devices, exchange(): lax.all_to_all(chunks, 'lon', 0, 0, axis_index_groups=[order], tiled=True)  24.3 us
    all_to_all x1, blocking collectives, gathered(): lax.all_to_all(copies, ('lat_0', 'lon'), 0, 0, axis_index_groups=[order],...  18.3 us
    all_to_all x1, starting transfers between devices, exchange(): lax.all_to_all(chunks, 'lon', 0, 0, axis_index_groups=[order], tiled=True)  17.2 us
    pallas_call x1, Pallas kernels, body(): pl.pallas_call(send_kernel, out_shape=jax.ShapeDtypeStruct((tiles * chunk...  1.95 us
    psum x1, blocking collectives, body(): sums = gathered(lax.psum(sums, 'lat_1'))  1.81 us
  transfers between devices with their start and end apart: 1, of which 1 were waited for; matrix products, arithmetic and copies ran while one was open for 0% of the time, Pallas kernels for 1%

profile of v7, /device:TPU:24, one launch (start us, length us, event | category | flops | bytes accessed | tf_op | source)
XLA Modules:
  0.0 66.4 jit_solution(2517913770605219556)
XLA Ops:
  0.6 2.0 %shard_map.95 = f32[1040,128]{1,0:T(8,128)} custom-call(s32[1,16]{1,0:T(1,128)} %route.1, f32[1,16,8,512]{3,2,1,0:T(8,128)} %flux.3, f32[1,16,512]{2,1,0:T(8,128)} %frac.3, s32[1,16,512]{2,1,0:T(8,128)} %mask.3, f32[1,16,512]{2,1,0:T(8,128)} %area.3), custom_call_target="tpu_custom_call" | custom-call | tf_op jit(solution)/shard_map/pallas_call | solution.py:171
  2.6 0.0 copy-start
  2.6 0.0 copy-start.1
  2.6 0.0 copy-start.2
  2.6 0.0 copy-start.3
  2.6 0.0 copy-start.4
  2.7 0.0 copy-start.5
  2.7 0.0 copy-start.6
  2.7 17.2 %all-to-all-start = ((f32[16,65,1,128]{3,2,1,0:T(1,128)}), f32[16,65,1,128]{3,2,1,0:T(1,128)S(1)}, u32[]{:S(2)}, u32[]{:S(2)}) async-start(f32[16,65,1,128]{3,2,1,0:T(1,128)} %bitcast.5), calls=%async_computation | async-start | bytes 1064960 | tf_op jit(solution)/shard_map/all_to_all | solution.py:150
  19.9 0.0 copy-done
  19.9 0.0 copy-done.1
  19.9 0.0 copy-done.2
  19.9 0.0 copy-done.3
  19.9 0.0 copy-done.4
  19.9 0.0 copy-done.5
  19.9 0.0 copy-done.6
  19.9 0.7 %shard_map.96 = (s32[1,128]{1,0:T(1,128)S(1)}, f32[1,128]{1,0:T(1,128)S(1)}) custom-call(s32[8]{0:T(128)S(1)} %copy-done.6, f32[1,16,8,512]{3,2,1,0:T(8,128)S(1)} %copy-done, f32[1,16,512]{2,1,0:T(8,128)S(1)} %copy-done.2, s32[1,16,512]{2,1,0:T(8,128)S(1)} %copy-done.3, f32[1,16,512]{2,1,0:T(8,128)S(1)} %copy-done.4, f32[64,128]{1,0:T(8,128)S(1)} %copy-done.5, ...), custom_call_target="tpu_custom_call" | custom-call | tf_op jit(solution)/shard_map/pallas_call | solution.py:188
  20.6 24.3 %all-to-all-done = f32[16,65,1,128]{3,2,1,0:T(1,128)S(1)} async-done(((f32[16,65,1,128]{3,2,1,0:T(1,128)}), f32[16,65,1,128]{3,2,1,0:T(1,128)S(1)}, u32[]{:S(2)}, u32[]{:S(2)}) %all-to-all-start) | async-done | bytes 532512 | tf_op jit(solution)/shard_map/all_to_all | solution.py:150
  44.9 0.3 shard_map.97
  45.3 1.8 %psum.7 = s32[128]{0:T(128)S(1)} all-reduce(s32[128]{0:T(128)S(1)} %bitcast.4), channel_id=1, replica_groups=mesh['member'=4,'lat_0'=4,'lat_1'=2,'lon'=16] {'lat_1'}, use_global_device_ids=true, to_apply=%region_0.0 | all-reduce | flops 128 | bytes 1024 | tf_op jit(solution)/shard_map/psum | solution.py:209
  47.1 18.3 %all_to_all.10.sums = s32[64,1,128]{2,1,0:T(1,128)S(1)} all-to-all(s32[64,1,128]{2,1,0:T(1,128)S(1)} %broadcast_in_dim.9), channel_id=1, replica_groups={{72,104,8,40,73,105,9,41,74,106,10,42,75,107,11,43,76,108,12,44,77,109,..., dimensions={0} | all-to-all | bytes 65536 | tf_op jit(solution)/shard_map/all_to_all | solution.py:159
  65.4 1.0 %shard_map.98 = (f32[8,64,128]{2,1,0:T(8,128)}, f32[8]{0:T(128)}) custom-call(s32[64,1,128]{2,1,0:T(1,128)S(1)} %all_to_all.10.sums, f32[1,128]{1,0:T(1,128)S(1)} %get-tuple-element.8.scaling, f32[8,64,128]{2,1,0:T(8,128)S(1)} %get-tuple-element.9.quotient, s32[64,128]{1,0:T(8,128)S(1)} %copy-done.1), custom_call_target="tpu_custom_call" | custom-call | tf_op jit(solution)/shard_map/pallas_call | solution.py:210
  (1 shorter events, 0.0 us)
Async XLA Ops:
  2.6 17.3 %copy-start = (f32[1,16,8,512]{3,2,1,0:T(8,128)S(1)}, f32[1,16,8,512]{3,2,1,0:T(8,128)}, u32[]{:S(2)}) copy-start(f32[1,16,8,512]{3,2,1,0:T(8,128)} %flux.3) | copy-start | bytes 786436
  2.6 17.3 %copy-start.1 = (s32[64,128]{1,0:T(8,128)S(1)}, s32[64,128]{1,0:T(8,128)}, u32[]{:S(2)}) copy-start(s32[64,128]{1,0:T(8,128)} %ocean_wet.5) | copy-start | bytes 98308
  2.6 17.3 %copy-start.2 = (f32[1,16,512]{2,1,0:T(8,128)S(1)}, f32[1,16,512]{2,1,0:T(8,128)}, u32[]{:S(2)}) copy-start(f32[1,16,512]{2,1,0:T(8,128)} %frac.3) | copy-start | bytes 98308
  2.6 17.3 %copy-start.3 = (s32[1,16,512]{2,1,0:T(8,128)S(1)}, s32[1,16,512]{2,1,0:T(8,128)}, u32[]{:S(2)}) copy-start(s32[1,16,512]{2,1,0:T(8,128)} %mask.3) | copy-start | bytes 98308
  2.6 17.3 %copy-start.4 = (f32[1,16,512]{2,1,0:T(8,128)S(1)}, f32[1,16,512]{2,1,0:T(8,128)}, u32[]{:S(2)}) copy-start(f32[1,16,512]{2,1,0:T(8,128)} %area.3) | copy-start | bytes 98308
  2.7 17.3 %copy-start.5 = (f32[64,128]{1,0:T(8,128)S(1)}, f32[64,128]{1,0:T(8,128)}, u32[]{:S(2)}) copy-start(f32[64,128]{1,0:T(8,128)} %ocean_area.3) | copy-start | bytes 98308
  2.7 17.3 %copy-start.6 = (s32[8]{0:T(128)S(1)}, s32[8]{0:T(128)}, u32[]{:S(2)}) copy-start(s32[8]{0:T(128)} %exponent.1) | copy-start | bytes 100
  2.7 42.2 %all-to-all-start = ((f32[16,65,1,128]{3,2,1,0:T(1,128)}), f32[16,65,1,128]{3,2,1,0:T(1,128)S(1)}, u32[]{:S(2)}, u32[]{:S(2)}) async-start(f32[16,65,1,128]{3,2,1,0:T(1,128)} %bitcast.5), calls=%async_computation | async-start | bytes 1064960 | tf_op jit(solution)/shard_map/all_to_all | solution.py:150
